TPU v7x, 32 devices: a whole 2x2x4 slice. The times are simulated.
32 devices in a mesh: group: 4 (over z), shard: 8 (over y, x, core).
Axes of the slice: x: 2, y: 2, z: 4, core: 2. Of those that a mesh axis runs over, the one named last changes fastest.
Arguments:
- features: bfloat16 [64, 512, 512], P(('group', 'shard')), may hold values from -6 to 6
- lengths: int32 [64], P(('group', 'shard')), may hold values from 128 to 512, as said below
- starts: int32 [64, 40], P(('group', 'shard')), may hold values from 0 to 511
- labels: int32 [64, 512], P(('group', 'shard')), may hold values from 0 to 499
- step_count: int32 [1], replicated, may hold values from 1 to 20
- weight_in: float32 [512, 768], P('shard'), may hold values from -0.25 to 0.25
- weight_rows: float32 [2, 768, 3072], P(None, 'shard'), may hold values from -0.21875 to 0.21875
- weight_down: float32 [3072, 768], P('shard'), may hold values from -0.109375 to 0.109375
- weight_head: float32 [1268, 256], P(None, 'shard'), may hold values from -0.21875 to 0.21875
- vectors: float32 [14, 3072], P(None, 'shard')
- moment_in: float32 [512, 768], P('shard'), may hold values from -5.722046e-06 to 5.722046e-06
- moment_rows: float32 [2, 768, 3072], P(None, 'shard'), may hold values from -5.722046e-06 to 5.722046e-06
- moment_down: float32 [3072, 768], P('shard'), may hold values from -5.722046e-06 to 5.722046e-06
- moment_head: float32 [1268, 256], P(None, 'shard'), may hold values from -5.722046e-06 to 5.722046e-06
- moment_vectors: float32 [14, 3072], P(None, 'shard'), may hold values from -5.722046e-06 to 5.722046e-06
- second_in: float32 [512, 768], P('shard'), may hold values from 1.2757185e-14 to 5.102874e-14
- second_rows: float32 [2, 768, 3072], P(None, 'shard'), may hold values from 1.2757185e-14 to 5.102874e-14
- second_down: float32 [3072, 768], P('shard'), may hold values from 1.2757185e-14 to 5.102874e-14
- second_head: float32 [1268, 256], P(None, 'shard'), may hold values from 1.2757185e-14 to 5.102874e-14
- second_vectors: float32 [14, 3072], P(None, 'shard'), may hold values from 1.2757185e-14 to 5.102874e-14
Outputs:
- new_weight_in: float32 [512, 768], P('shard')
- new_weight_rows: float32 [2, 768, 3072], P(None, 'shard')
- new_weight_down: float32 [3072, 768], P('shard')
- new_weight_head: float32 [1268, 256], P(None, 'shard')
- new_vectors: float32 [14, 3072], P(None, 'shard')
- new_moment_in: float32 [512, 768], P('shard')
- new_moment_rows: float32 [2, 768, 3072], P(None, 'shard')
- new_moment_down: float32 [3072, 768], P('shard')
- new_moment_head: float32 [1268, 256], P(None, 'shard')
- new_moment_vectors: float32 [14, 3072], P(None, 'shard')
- new_second_in: float32 [512, 768], P('shard')
- new_second_rows: float32 [2, 768, 3072], P(None, 'shard')
- new_second_down: float32 [3072, 768], P('shard')
- new_second_head: float32 [1268, 256], P(None, 'shard')
- new_second_vectors: float32 [14, 3072], P(None, 'shard')
- copy_in: bfloat16 [512, 768], P('shard')
- copy_rows: bfloat16 [2, 768, 3072], P(None, 'shard')
- copy_down: bfloat16 [3072, 768], P('shard')
- copy_head: bfloat16 [1268, 256], P(None, 'shard')
- copy_vectors: bfloat16 [14, 3072], P(None, 'shard')
- loss_value: float32 [1], replicated
- grad_norm: float32 [1], replicated
Inputs may be any that keep to these rules, and one draw needn't show every extreme that they name: `lengths`: utterance 0 has exactly 512 valid frames.
All inputs are finite; a program needn't handle non-finite values.
Results may differ from a plain program's by a relative error of at most 0.004.
The roundings to bfloat16 on the way count: a program that leaves them out, or rounds other values in their place, can miss the bound.
Values may be sent and summed in bfloat16 or wider, within the bound.
A program may use at most 256 MiB of HBM per device.

v0:
```python
import jax
import jax.numpy as jnp
from jax import lax
from jax.sharding import PartitionSpec as P

D = 768
CH = 512
HEADS = 12
HEAD_DIM = 64
FF = 3072
CD = 256
CODES = 500
LEN = 512
SPAN = 10


beta_one = 0.9
beta_two = 0.999
rate = 0.03
decay = 0.01
adam_eps = 1e-08
clip_norm = 0.01
temper = 10.0


def product(left, right):
    return jnp.dot(left, right, preferred_element_type=jnp.float32)


def layer_norm(values, gain, shift):
    centred = values - jnp.mean(values, -1, keepdims=True)
    return (
        centred * lax.rsqrt(jnp.mean(centred * centred, -1, keepdims=True) + 1e-05) * gain + shift
    )


def unit_rows(values):
    return values * lax.rsqrt(jnp.sum(values * values, -1, keepdims=True) + 1e-06)


def gelu_exact(values):
    return jax.nn.gelu(values, approximate=False)


def widen(row):
    return jnp.pad(row, (0, FF - row.shape[0]))


def span_mask(length, begins):
    position = jnp.arange(LEN, dtype=jnp.int32)
    first = begins % (length - SPAN + 1)
    inside = (position[None, :] >= first[:, None]) & (position[None, :] < first[:, None] + SPAN)
    return jnp.any(inside, 0) & (position < length)


def attention_probs(triple, valid, logsum):
    query = triple[:, :D].reshape(LEN, HEADS, HEAD_DIM)
    keys = triple[:, D : 2 * D].reshape(LEN, HEADS, HEAD_DIM)
    scores = jnp.einsum(
        "qhd,khd->hqk", query, keys, preferred_element_type=jnp.float32
    ) * HEAD_DIM ** (-0.5)
    scores = jnp.where(valid[None, None, :], scores, -1e30)
    if logsum is None:
        highest_score = jnp.max(scores, -1, keepdims=True)
        logsum = highest_score + jnp.log(
            jnp.sum(jnp.exp(scores - highest_score), -1, keepdims=True)
        )
    return (jnp.exp(scores - logsum), logsum)


def forward(weights, codes_unit, frames, length, masked, label_row):
    w_input, w_block, w_lower, w_final, vecs_low = weights
    vecs = vecs_low.astype(jnp.float32)
    valid = jnp.arange(LEN, dtype=jnp.int32) < length
    frames32 = frames.astype(jnp.float32)
    normed = layer_norm(frames32, vecs[0, :CH], vecs[1, :CH]).astype(jnp.bfloat16)
    hidden = product(normed, w_input) + vecs[2, :D]
    hidden = jnp.where(masked[:, None], vecs[3, :D][None, :], hidden)
    hid_low = hidden.astype(jnp.bfloat16)
    bias_qkv = jnp.concatenate([vecs[4, :D], jnp.zeros((D,), jnp.float32), vecs[5, :D]])
    triple = (product(hid_low, w_block[0, :, : 3 * D]) + bias_qkv).astype(jnp.bfloat16)
    probs, logsum = attention_probs(triple, valid, None)
    values = triple[:, 2 * D :].reshape(LEN, HEADS, HEAD_DIM)
    attended = (
        jnp.einsum(
            "hqk,khd->qhd", probs.astype(jnp.bfloat16), values, preferred_element_type=jnp.float32
        )
        .reshape(LEN, D)
        .astype(jnp.bfloat16)
    )
    resid_one = hidden + product(attended, w_block[0, :, 3 * D :]) + vecs[6, :D]
    first = layer_norm(resid_one, vecs[7, :D], vecs[8, :D])
    first_low = first.astype(jnp.bfloat16)
    before = product(first_low, w_block[1]) + vecs[9]
    active = gelu_exact(before).astype(jnp.bfloat16)
    resid_two = first + product(active, w_lower) + vecs[10, :D]
    second_low = layer_norm(resid_two, vecs[11, :D], vecs[12, :D]).astype(jnp.bfloat16)
    head = product(second_low, w_final[:D]) + vecs[13, :CD]
    head_unit = unit_rows(head).astype(jnp.bfloat16)
    logits = temper * product(head_unit, codes_unit.T)
    onehot = label_row[:, None] == jnp.arange(CODES, dtype=jnp.int32)[None, :]
    picked = jnp.sum(jnp.where(onehot, logits, 0.0), -1)
    losses = jax.nn.logsumexp(logits, -1) - picked
    loss_sum = jnp.sum(jnp.where(masked, losses, 0.0))
    kept = (
        frames32,
        normed,
        hidden,
        hid_low,
        triple,
        logsum,
        attended,
        resid_one,
        first,
        first_low,
        before,
        active,
        resid_two,
        second_low,
        head,
        head_unit,
        logits,
        onehot,
        valid,
    )
    return (loss_sum, kept)


def backward(weights, codes_unit, masked, kept, scale):
    w_input, w_block, w_lower, w_final, vecs_low = weights
    vecs = vecs_low.astype(jnp.float32)
    (
        frames32,
        normed,
        hidden,
        hid_low,
        triple,
        logsum,
        attended,
        resid_one,
        first,
        first_low,
        before,
        active,
        resid_two,
        second_low,
        head,
        head_unit,
        logits,
        onehot,
        valid,
    ) = kept
    chances = jax.nn.softmax(logits, -1)
    d_logit = (
        temper * (jnp.where(masked[:, None], chances - onehot.astype(jnp.float32), 0.0) * scale)
    ).astype(jnp.bfloat16)
    d_codes_unit = product(d_logit.T, head_unit)
    _, unit_back = jax.vjp(unit_rows, head)
    d_head = unit_back(product(d_logit, codes_unit))[0].astype(jnp.bfloat16)
    g_final = product(second_low.T, d_head)
    d_second = product(d_head, w_final[:D].T)
    _, norm_two_back = jax.vjp(layer_norm, resid_two, vecs[11, :D], vecs[12, :D])
    d_resid_two, g_gain_two, g_shift_two = norm_two_back(d_second)
    d_lower = d_resid_two.astype(jnp.bfloat16)
    g_lower = product(active.T, d_lower)
    _, gelu_back = jax.vjp(gelu_exact, before)
    d_before = gelu_back(product(d_lower, w_lower.T))[0].astype(jnp.bfloat16)
    g_up = product(first_low.T, d_before)
    d_first = d_resid_two + product(d_before, w_block[1].T)
    _, norm_one_back = jax.vjp(layer_norm, resid_one, vecs[7, :D], vecs[8, :D])
    d_resid_one, g_gain_one, g_shift_one = norm_one_back(d_first)
    d_branch = d_resid_one.astype(jnp.bfloat16)
    g_output = product(attended.T, d_branch)
    d_attended = (
        product(d_branch, w_block[0, :, 3 * D :].T)
        .astype(jnp.bfloat16)
        .reshape(LEN, HEADS, HEAD_DIM)
    )
    probs, _ = attention_probs(triple, valid, logsum)
    query = triple[:, :D].reshape(LEN, HEADS, HEAD_DIM)
    keys = triple[:, D : 2 * D].reshape(LEN, HEADS, HEAD_DIM)
    values = triple[:, 2 * D :].reshape(LEN, HEADS, HEAD_DIM)
    g_values = jnp.einsum(
        "hqk,qhd->khd", probs.astype(jnp.bfloat16), d_attended, preferred_element_type=jnp.float32
    )
    d_probs = jnp.einsum("qhd,khd->hqk", d_attended, values, preferred_element_type=jnp.float32)
    d_scores = probs * (d_probs - jnp.sum(probs * d_probs, -1, keepdims=True))
    d_scores = (d_scores * HEAD_DIM ** (-0.5)).astype(jnp.bfloat16)
    g_query = jnp.einsum("hqk,khd->qhd", d_scores, keys, preferred_element_type=jnp.float32)
    g_keys = jnp.einsum("hqk,qhd->khd", d_scores, query, preferred_element_type=jnp.float32)
    d_triple = jnp.concatenate(
        [g_query.reshape(LEN, D), g_keys.reshape(LEN, D), g_values.reshape(LEN, D)], 1
    ).astype(jnp.bfloat16)
    g_triple = product(hid_low.T, d_triple)
    triple_sums = jnp.sum(d_triple.astype(jnp.float32), 0)
    d_hidden = d_resid_one + product(d_triple, w_block[0, :, : 3 * D].T)
    g_mask = jnp.sum(jnp.where(masked[:, None], d_hidden, 0.0), 0)
    d_proj = jnp.where(masked[:, None], 0.0, d_hidden).astype(jnp.bfloat16)
    g_input = product(normed.T, d_proj)
    _, norm_in_back = jax.vjp(layer_norm, frames32, vecs[0, :CH], vecs[1, :CH])
    _, g_gain_in, g_shift_in = norm_in_back(product(d_proj, w_input.T))
    rows = [
        g_gain_in,
        g_shift_in,
        jnp.sum(d_proj.astype(jnp.float32), 0),
        g_mask,
        triple_sums[:D],
        triple_sums[2 * D :],
        jnp.sum(d_branch.astype(jnp.float32), 0),
        g_gain_one,
        g_shift_one,
        jnp.sum(d_before.astype(jnp.float32), 0),
        jnp.sum(d_lower.astype(jnp.float32), 0),
        g_gain_two,
        g_shift_two,
        jnp.sum(d_head.astype(jnp.float32), 0),
    ]
    g_vectors = jnp.stack([widen(row) for row in rows])
    g_block = jnp.stack([jnp.concatenate([g_triple, g_output], 1), g_up])
    return (g_input, g_block, g_lower, g_final, d_codes_unit, g_vectors)


def per_device(
    features,
    lengths,
    starts,
    labels,
    step_count,
    weight_in,
    weight_rows,
    weight_down,
    weight_head,
    vectors,
    moment_in,
    moment_rows,
    moment_down,
    moment_head,
    moment_vectors,
    second_in,
    second_rows,
    second_down,
    second_head,
    second_vectors,
):
    masters = (weight_in, weight_rows, weight_down, weight_head, vectors)
    moments = (moment_in, moment_rows, moment_down, moment_head, moment_vectors)
    seconds = (second_in, second_rows, second_down, second_head, second_vectors)
    low_shards = tuple((w.astype(jnp.bfloat16) for w in masters))
    gathered = (
        lax.all_gather(low_shards[0], "shard", axis=0, tiled=True),
        lax.all_gather(low_shards[1], "shard", axis=1, tiled=True),
        lax.all_gather(low_shards[2], "shard", axis=0, tiled=True),
        lax.all_gather(low_shards[3], "shard", axis=1, tiled=True),
        lax.all_gather(low_shards[4], "shard", axis=1, tiled=True),
    )
    codes_unit = unit_rows(gathered[3][D:].astype(jnp.float32)).astype(jnp.bfloat16)
    masks, kept_all = ([], [])
    local_loss = jnp.zeros((), jnp.float32)
    local_count = jnp.zeros((), jnp.float32)
    for utter in range(features.shape[0]):
        masked = span_mask(lengths[utter], starts[utter])
        loss_sum, kept = forward(
            gathered, codes_unit, features[utter], lengths[utter], masked, labels[utter]
        )
        masks.append(masked)
        kept_all.append(kept)
        local_loss = local_loss + loss_sum
        local_count = local_count + jnp.sum(masked.astype(jnp.float32))
    totals = lax.psum((local_count, local_loss), ("group", "shard"))
    count = totals[0]
    loss = totals[1] / count
    again = (
        lax.all_gather(low_shards[0], "shard", axis=0, tiled=True),
        lax.all_gather(low_shards[1], "shard", axis=1, tiled=True),
        lax.all_gather(low_shards[2], "shard", axis=0, tiled=True),
        lax.all_gather(low_shards[3], "shard", axis=1, tiled=True),
        lax.all_gather(low_shards[4], "shard", axis=1, tiled=True),
    )
    scale = 1.0 / count
    grads = None
    for utter in range(features.shape[0]):
        part_grads = backward(again, codes_unit, masks[utter], kept_all[utter], scale)
        grads = part_grads if grads is None else jax.tree.map(jnp.add, grads, part_grads)
    g_input, g_block, g_lower, g_final, d_codes_unit, g_vectors = grads
    _, codes_back = jax.vjp(unit_rows, again[3][D:].astype(jnp.float32))
    g_codes = codes_back(d_codes_unit)[0]
    full = (g_input, g_block, g_lower, jnp.concatenate([g_final, g_codes], 0), g_vectors)
    pooled = lax.psum((full[0], full[1], full[2], full[3], full[4]), "group")
    summed = (
        lax.psum_scatter(pooled[0], "shard", scatter_dimension=0, tiled=True),
        lax.psum_scatter(pooled[1], "shard", scatter_dimension=1, tiled=True),
        lax.psum_scatter(pooled[2], "shard", scatter_dimension=0, tiled=True),
        lax.psum_scatter(pooled[3], "shard", scatter_dimension=1, tiled=True),
        lax.psum_scatter(pooled[4], "shard", scatter_dimension=1, tiled=True),
    )
    local_squares = sum((jnp.sum(g * g) for g in summed))
    norm = jnp.sqrt(lax.psum(local_squares, "shard"))
    factor = jnp.minimum(1.0, clip_norm / (norm + 1e-06))
    steps = step_count[0].astype(jnp.float32)
    fix_one = 1.0 - jnp.power(beta_one, steps)
    fix_two = 1.0 - jnp.power(beta_two, steps)
    decays = (decay, decay, decay, decay, 0.0)
    new_w, new_m, new_v = ([], [], [])
    for weight, grad, moment, square, shrink in zip(masters, summed, moments, seconds, decays):
        grad = grad * factor
        moment = beta_one * moment + (1.0 - beta_one) * grad
        square = beta_two * square + (1.0 - beta_two) * grad * grad
        stepped = moment / fix_one / (jnp.sqrt(square / fix_two) + adam_eps)
        new_w.append(weight - rate * (stepped + shrink * weight))
        new_m.append(moment)
        new_v.append(square)
    copies = [w.astype(jnp.bfloat16) for w in new_w]
    return (
        new_w[0],
        new_w[1],
        new_w[2],
        new_w[3],
        new_w[4],
        new_m[0],
        new_m[1],
        new_m[2],
        new_m[3],
        new_m[4],
        new_v[0],
        new_v[1],
        new_v[2],
        new_v[3],
        new_v[4],
        copies[0],
        copies[1],
        copies[2],
        copies[3],
        copies[4],
        jnp.reshape(loss, (1,)),
        jnp.reshape(norm, (1,)),
    )


def solution(mesh):
    in_specs = (
        P(("group", "shard"), None, None),
        P(("group", "shard")),
        P(("group", "shard"), None),
        P(("group", "shard"), None),
        P(),
        P("shard", None),
        P(None, "shard", None),
        P("shard", None),
        P(None, "shard"),
        P(None, "shard"),
        P("shard", None),
        P(None, "shard", None),
        P("shard", None),
        P(None, "shard"),
        P(None, "shard"),
        P("shard", None),
        P(None, "shard", None),
        P("shard", None),
        P(None, "shard"),
        P(None, "shard"),
    )
    out_specs = (
        P("shard", None),
        P(None, "shard", None),
        P("shard", None),
        P(None, "shard"),
        P(None, "shard"),
        P("shard", None),
        P(None, "shard", None),
        P("shard", None),
        P(None, "shard"),
        P(None, "shard"),
        P("shard", None),
        P(None, "shard", None),
        P("shard", None),
        P(None, "shard"),
        P(None, "shard"),
        P("shard", None),
        P(None, "shard", None),
        P("shard", None),
        P(None, "shard"),
        P(None, "shard"),
        P(),
        P(),
    )
    return jax.shard_map(
        per_device, mesh=mesh, in_specs=in_specs, out_specs=out_specs, check_vma=False
    )
```

profile of v0, /device:TPU:0, one launch (start us, length us, event | category | flops | bytes accessed | tf_op | source)
XLA Modules:
  0.0 919.4 jit_solution(17438754244939763855)
XLA Ops:
  14.6 10.7 %all_gather.20 = bf16[14,3072]{1,0:T(8,128)(2,1)S(1)} all-gather(bf16[14,384]{1,0:T(8,128)(2,1)S(1)} %convert_element_type.260), channel_id=1, replica_groups=mesh['group'=4,'shard'=8] {'shard'}, dimensions={1}, use_global_device_ids=true | all-gather | bytes 96768 | tf_op jit(solution)/shard_map/all_gather | solution.py:254
  29.6 11.2 %all_gather.24 = bf16[1268,256]{0,1:T(8,128)(2,1)S(1)} all-gather(bf16[1268,32]{0,1:T(8,128)(2,1)S(1)} %convert_element_type.275), channel_id=1, replica_groups=mesh['group'=4,'shard'=8] {'shard'}, dimensions={1}, use_global_device_ids=true | all-gather | bytes 730368 | tf_op jit(solution)/shard_map/all_gather | solution.py:253
  42.6 14.5 %all_gather.21 = bf16[512,768]{1,0:T(8,128)(2,1)S(1)} all-gather(bf16[64,768]{1,0:T(8,128)(2,1)S(1)} %convert_element_type.263), channel_id=1, replica_groups=mesh['group'=4,'shard'=8] {'shard'}, dimensions={0}, use_global_device_ids=true | all-gather | bytes 884736 | tf_op jit(solution)/shard_map/all_gather | solution.py:250
  59.7 17.0 %all-gather.3.cloned.1.call-done = bf16[2,768,3072]{2,1,0:T(8,128)(2,1)} async-done(((bf16[2,96,3072]{2,1,0:T(8,128)(2,1)}), bf16[2,768,3072]{2,1,0:T(8,128)(2,1)}) %all-gather.3.cloned.1.call-update) | async-done | bytes 9437200 | tf_op jit(solution)/shard_map/all_gather | solution.py:251
  99.5 10.6 %fusion.17 = bf16[12,512,512]{1,2,0:T(8,128)(2,1)} fusion(f32[12,512,512]{1,2,0:T(8,128)} %copy-done, f32[12,512]{1,0:T(8,128)S(1)} %log_add_fusion, pred[512]{0:T(512)(128)(4,1)S(1)} %iota_compare_fusion.6), kind=kLoop, calls=%fused_computation.24 | loop fusion | flops 12582912 | bytes 18899456 | tf_op jit(solution)/shard_map/convert_element_type | solution.py:86
  124.4 10.1 %fusion.10 = bf16[12,512,512]{1,2,0:T(8,128)(2,1)} fusion(f32[12,512,512]{1,2,0:T(8,128)} %copy-done.1, f32[12,512]{1,0:T(8,128)S(1)} %log_add_fusion.1, pred[512]{0:T(512)(128)(4,1)S(1)} %iota_compare_fusion.7), kind=kLoop, calls=%fused_computation.21 | loop fusion | flops 12582912 | bytes 18899456 | tf_op jit(solution)/shard_map/convert_element_type | solution.py:86
  147.8 32.8 %multiply_convert_fusion.2 = (bf16[512,3072]{1,0:T(8,128)(2,1)}, f32[512,3072]{1,0:T(8,128)}, bf16[512,3072]{1,0:T(8,128)(2,1)}, f32[512,3072]{1,0:T(8,128)}, f32[512,3072]{1,0:T(8,128)}) fusion(f32[3072]{0:T(1024)S(1)} %bitcast.308, f32[512,3072]{1,0:T(8,128)S(1)} %fusion.73, bf16[2,768,3072]{2,1,0:T(8,128)(2,1)S(1)} %bitcast.321, ...), kind=kOutput, calls=%fused_computation.32 | convolution fusion | flops 2625503232 | bytes 37773312 | tf_op jit(solution)/shard_map/dot_general | solution.py:27
  180.7 6.6 fusion.206
  201.5 39.7 %all-reduce.26 = (f32[]{:T(128)}, f32[]{:T(128)}) all-reduce(f32[]{:T(128)S(6)} %add.567, f32[]{:T(128)S(6)} %add.626), channel_id=1, replica_groups=mesh['group'=4,'shard'=8] {'group','shard'}, use_global_device_ids=true, to_apply=%region_16.17 | all-reduce | flops 2 | bytes 16 | tf_op jit(solution)/shard_map/psum | solution.py:269
  262.5 18.0 %convert_reduce_fusion = (f32[3072]{0:T(1024)}, bf16[512,3072]{1,0:T(8,128)(2,1)}, f32[3072]{0:T(1024)}, bf16[512,3072]{1,0:T(8,128)(2,1)}) fusion(f32[512,3072]{1,0:T(8,128)} %get-tuple-element.205, f32[512,3072]{1,0:T(8,128)} %get-tuple-element.254, f32[3072]{0:T(1024)S(1)} %bitcast.309, f32[512,3072]{1,0:T(8,128)} %fusion.210, ...), kind=kOutput, calls=%fused_computation.29 | convolution fusion | flops 2469390336 | bytes 43290624 | tf_op jit(solution)/shard_map/dot_general | solution.py:27
  313.5 20.5 %fusion.83 = bf16[12,64,512]{2,1,0:T(8,128)(2,1)} fusion(bf16[512,12,64]{0,2,1:T(8,128)(2,1)} %bitcast.261, f32[12,512,512]{1,2,0:T(8,128)} %fusion.211, f32[12,512,512]{1,2,0:T(8,128)} %copy-done.1, f32[12,512]{1,0:T(8,128)S(1)} %copy-done.90, pred[512]{0:T(512)(128)(4,1)S(1)} %copy-done.125), kind=kOutput, calls=%fused_computation.151 | convolution fusion | flops 437656064 | bytes 26763776 | tf_op jit(solution)/shard_map/hqk,khd->qhd/dot_general | solution.py:189
  334.0 20.7 %fusion.86 = bf16[12,64,512]{2,1,0:T(8,128)(2,1)} fusion(bf16[512,12,64]{0,2,1:T(8,128)(2,1)} %bitcast.259, f32[12,512,512]{1,2,0:T(8,128)} %fusion.211, f32[12,512,512]{1,2,0:T(8,128)} %copy-done.1, f32[12,512]{1,0:T(8,128)S(1)} %copy-done.90, pred[512]{0:T(512)(128)(4,1)S(1)} %copy-done.125), kind=kOutput, calls=%fused_computation.152 | convolution fusion | flops 437656064 | bytes 26763776 | tf_op jit(solution)/shard_map/hqk,qhd->khd/dot_general | solution.py:190
  371.4 21.3 %fusion.77 = bf16[12,64,512]{2,1,0:T(8,128)(2,1)} fusion(bf16[512,12,64]{0,2,1:T(8,128)(2,1)} %bitcast.258, f32[12,512,512]{1,2,0:T(8,128)} %fusion.212, f32[12,512,512]{1,2,0:T(8,128)} %copy-done, f32[12,512]{1,0:T(8,128)S(1)} %copy-done.88, pred[512]{0:T(512)(128)(4,1)S(1)} %copy-done.123), kind=kOutput, calls=%fused_computation.149 | convolution fusion | flops 437656064 | bytes 26763776 | tf_op jit(solution)/shard_map/hqk,khd->qhd/dot_general | solution.py:189
  399.1 19.9 %fusion.80 = bf16[12,64,512]{2,1,0:T(8,128)(2,1)S(1)} fusion(bf16[512,12,64]{0,2,1:T(8,128)(2,1)} %bitcast.256, f32[12,512,512]{1,2,0:T(8,128)} %fusion.212, f32[12,512,512]{1,2,0:T(8,128)} %copy-done, f32[12,512]{1,0:T(8,128)S(1)} %copy-done.88, pred[512]{0:T(512)(128)(4,1)S(1)} %copy-done.123), kind=kOutput, calls=%fused_computation.150 | convolution fusion | flops 437656064 | bytes 26763776 | tf_op jit(solution)/shard_map/hqk,qhd->khd/dot_general | solution.py:190
  457.3 8.1 maximum_bitcast_fusion.1
  465.3 8.3 maximum_bitcast_fusion
  479.1 10.1 %convolution_bitcast_fusion = f32[1,768,3072]{2,1,0:T(8,128)} fusion(bf16[512,3072]{1,0:T(8,128)(2,1)} %get-tuple-element.181, f32[512,768]{1,0:T(8,128)S(1)} %copy-done.33, f32[512]{0:T(512)S(1)} %fusion.139, f32[512]{0:T(512)S(1)} %broadcast_multiply_fusion.1, f32[768]{0:T(1024)S(1)} %get-tuple-element.139, f32[768]{0:T(1024)S(1)} %get-tuple-element.140), kind=kOutput, calls=%fused_computation.77 | convolution fusion | flops 2417885184 | bytes 14166016 | tf_op jit(solution)/shard_map/dot_general | solution.py:27
  489.3 11.9 %maximum_add_fusion = f32[2,768,3072]{2,1,0:T(8,128)} fusion(f32[1,768,3072]{2,1,0:T(8,128)S(1)} %convolution_bitcast_fusion.1, f32[1,768,3072]{2,1,0:T(8,128)S(1)} %bitcast.235, f32[1,768,3072]{2,1,0:T(8,128)} %convolution_bitcast_fusion, f32[1,768,3072]{2,1,0:T(8,128)S(1)} %bitcast.233), kind=kLoop, calls=%fused_computation.2 | loop fusion | flops 14155776 | bytes 56623104 | tf_op jit(solution)/shard_map/add | solution.py:283
  515.4 36.1 %reduce-scatter.12.cloned.1.call-done = f32[384,768]{1,0:T(8,128)} async-done(((f32[3072,768]{1,0:T(8,128)}), f32[384,768]{1,0:T(8,128)}) %reduce-scatter.12.cloned.1.call-update) | async-done | bytes 1179664 | tf_op jit(solution)/shard_map/reduce_scatter | solution.py:292
  551.5 129.6 %reduce-scatter.10.cloned.1.call-done = f32[2,96,3072]{2,1,0:T(8,128)} async-done(((f32[2,768,3072]{2,1,0:T(8,128)}), f32[2,96,3072]{2,1,0:T(8,128)}) %reduce-scatter.10.cloned.1.call-update) | async-done | bytes 2359312 | tf_op jit(solution)/shard_map/reduce_scatter | solution.py:291
  682.0 35.4 %reduce-scatter.14.cloned.1.call-done = f32[14,384]{1,0:T(8,128)} async-done(((f32[14,3072]{1,0:T(8,128)}), f32[14,384]{1,0:T(8,128)}) %reduce-scatter.14.cloned.1.call-update) | async-done | bytes 21520 | tf_op jit(solution)/shard_map/reduce_scatter | solution.py:294
  717.4 20.2 %psum.68 = f32[14,384]{1,0:T(8,128)S(1)} all-reduce(f32[14,384]{1,0:T(8,128)} %reduce-scatter.14.cloned.1.call-done), channel_id=1, replica_groups=mesh['group'=4,'shard'=8] {'group'}, use_global_device_ids=true, to_apply=%region_79.80 | all-reduce | flops 5376 | bytes 43008 | tf_op jit(solution)/shard_map/psum | solution.py:288
  738.3 128.7 %all-reduce.30.cloned.1.call-done = (f32[64,768]{1,0:T(8,128)}, f32[2,96,3072]{2,1,0:T(8,128)}, f32[384,768]{1,0:T(8,128)}, f32[1268,32]{0,1:T(8,128)}) async-done(((f32[64,768]{1,0:T(8,128)}, f32[2,96,3072]{2,1,0:T(8,128)}, f32[384,768]{1,0:T(8,128)}, f32[1268,32]{0,1:T(8,128)}), (f32[64,768]{1,0:T(8,128)}, f32[2,96,3072]{2,1,0:T(8,128)}, f32[384,768]{1,0:T(8,128)}, ...) | async-done | bytes 3897872 | tf_op jit(solution)/shard_map/psum | solution.py:288
  879.8 14.2 %psum.62 = f32[]{:T(128)} all-reduce(f32[]{:T(128)S(6)} %add.597), channel_id=1, replica_groups=mesh['group'=4,'shard'=8] {'shard'}, use_global_device_ids=true, to_apply=%region_82.83 | all-reduce | flops 1 | bytes 8 | tf_op jit(solution)/shard_map/psum | solution.py:297
  (529 shorter events, 233.6 us)
Async XLA Ops:
  7.3 69.5 %all-gather.3.cloned.1.call-start = ((), (), s32[]{:S(2)}) async-start(), calls=%async_computation.5 | async-start | bytes 10616832 | tf_op jit(solution)/shard_map/all_gather | solution.py:251
  10.3 170.3 %all-gather.5.cloned.1.call-start = ((), (), s32[]{:S(2)}) async-start(), calls=%async_computation.6 | async-start | bytes 5308416 | tf_op jit(solution)/shard_map/all_gather | solution.py:252
  11.3 504.1 %reduce-scatter.16.cloned.1.call-start = ((), (), s32[]{:S(2)}) async-start(), calls=%async_computation.11 | async-start | bytes 1474560
  12.6 86.9 %copy-start.122 = (pred[512]{0:T(512)(128)(4,1)}, pred[512]{0:T(512)(128)(4,1)S(1)}, u32[]{:S(2)}) copy-start(pred[512]{0:T(512)(128)(4,1)S(1)} %iota_compare_fusion.6) | copy-start | bytes 1540
  14.6 109.8 %copy-start.124 = (pred[512]{0:T(512)(128)(4,1)}, pred[512]{0:T(512)(128)(4,1)S(1)}, u32[]{:S(2)}) copy-start(pred[512]{0:T(512)(128)(4,1)S(1)} %iota_compare_fusion.7) | copy-start | bytes 1540
  25.8 33.1 %copy-start.118 = (f32[1,512]{1,0:T(1,128)}, f32[1,512]{1,0:T(1,128)S(1)}, u32[]{:S(2)}) copy-start(f32[1,512]{1,0:T(1,128)S(1)} %get-tuple-element.220) | copy-start | bytes 6148
  25.8 33.1 %copy-start.120 = (f32[1,512]{1,0:T(1,128)}, f32[1,512]{1,0:T(1,128)S(1)}, u32[]{:S(2)}) copy-start(f32[1,512]{1,0:T(1,128)S(1)} %get-tuple-element.221) | copy-start | bytes 6148
  26.8 32.1 %copy-start.145 = (pred[512]{0:T(512)(128)(4,1)}, pred[512]{0:T(512)(128)(4,1)S(1)}, u32[]{:S(2)}) copy-start(pred[512]{0:T(512)(128)(4,1)S(1)} %fusion.161) | copy-start | bytes 1540
  27.5 31.4 %copy-start.143 = (pred[512]{0:T(512)(128)(4,1)}, pred[512]{0:T(512)(128)(4,1)S(1)}, u32[]{:S(2)}) copy-start(pred[512]{0:T(512)(128)(4,1)S(1)} %fusion.162) | copy-start | bytes 1540
  28.4 28.7 %copy-start.99 = (f32[512]{0:T(512)}, f32[512]{0:T(512)S(1)}, u32[]{:S(2)}) copy-start(f32[512]{0:T(512)S(1)} %get-tuple-element.277) | copy-start | bytes 6148
  28.4 31.3 %copy-start.115 = (f32[512]{0:T(512)}, f32[512]{0:T(512)S(1)}, u32[]{:S(2)}) copy-start(f32[512]{0:T(512)S(1)} %get-tuple-element.278) | copy-start | bytes 6148
  28.9 28.2 %copy-start.112 = (f32[512]{0:T(512)}, f32[512]{0:T(512)S(1)}, u32[]{:S(2)}) copy-start(f32[512]{0:T(512)S(1)} %add_rsqrt_fusion) | copy-start | bytes 6148
  29.0 30.7 %copy-start.133 = (f32[512]{0:T(512)}, f32[512]{0:T(512)S(1)}, u32[]{:S(2)}) copy-start(f32[512]{0:T(512)S(1)} %add_rsqrt_fusion.1) | copy-start | bytes 6148
  83.5 51.0 %copy-start.6 = (bf16[512,768]{0,1:T(8,128)(2,1)}, bf16[512,768]{0,1:T(8,128)(2,1)S(1)}, u32[]{:S(2)}) copy-start(bf16[512,768]{0,1:T(8,128)(2,1)S(1)} %copy.174) | copy-start | bytes 2359300
  116.8 28.4 %copy-start.31 = (f32[512,768]{1,0:T(8,128)}, f32[512,768]{1,0:T(8,128)S(1)}, u32[]{:S(2)}) copy-start(f32[512,768]{1,0:T(8,128)S(1)} %get-tuple-element.249) | copy-start | bytes 4718596
  193.2 48.6 %copy-start.146 = (pred[512]{0:T(512)(128)(4,1)S(1)}, pred[512]{0:T(512)(128)(4,1)}, u32[]{:S(2)}) copy-start(pred[512]{0:T(512)(128)(4,1)} %copy-done.145) | copy-start | bytes 1540
  361.3 154.1 %reduce-scatter.8.cloned.1.call-start = ((), (), s32[]{:S(2)}) async-start(), calls=%async_computation.7 | async-start | bytes 1769472 | tf_op jit(solution)/shard_map/reduce_scatter | solution.py:290
  432.0 119.4 %reduce-scatter.12.cloned.1.call-start = ((), (), s32[]{:S(2)}) async-start(), calls=%async_computation.9 | async-start | bytes 10616832 | tf_op jit(solution)/shard_map/reduce_scatter | solution.py:292
  442.5 238.6 %reduce-scatter.10.cloned.1.call-start = ((), (), s32[]{:S(2)}) async-start(), calls=%async_computation.8 | async-start | bytes 21233664 | tf_op jit(solution)/shard_map/reduce_scatter | solution.py:291
  501.4 216.1 %reduce-scatter.14.cloned.1.call-start = ((), (), s32[]{:S(2)}) async-start(), calls=%async_computation.10 | async-start | bytes 221184 | tf_op jit(solution)/shard_map/reduce_scatter | solution.py:294
  515.3 351.6 %all-reduce.30.cloned.1.call-start = ((), (), s32[]{:S(2)}) async-start(), calls=%async_computation.12 | async-start | bytes 7798784 | tf_op jit(solution)/shard_map/psum | solution.py:288
  681.1 219.3 %copy-start.43 = (f32[384,768]{1,0:T(8,128)S(1)}, f32[384,768]{1,0:T(8,128)}, u32[]{:S(2)}) copy-start(f32[384,768]{1,0:T(8,128)} %param.27) | copy-start | bytes 3538948
  681.1 219.3 %copy-start.77 = (f32[384,768]{1,0:T(8,128)S(1)}, f32[384,768]{1,0:T(8,128)}, u32[]{:S(2)}) copy-start(f32[384,768]{1,0:T(8,128)} %param.37) | copy-start | bytes 3538948
  866.9 33.5 %copy-start.44 = (f32[384,768]{1,0:T(8,128)S(1)}, f32[384,768]{1,0:T(8,128)}, u32[]{:S(2)}) copy-start(f32[384,768]{1,0:T(8,128)} %get-tuple-element.154) | copy-start | bytes 3538948
  (148 other events, 1090.3 us)
Sparse Core Ops, SparseCore 0:
  10.6 66.1 all-gather.2
  79.2 38.9 all-gather.4
  361.5 38.2 reduce-scatter.15
  432.2 39.3 reduce-scatter.7
  474.9 76.4 reduce-scatter.11
  555.0 126.1 reduce-scatter.9
  684.7 32.6 reduce-scatter.13
  720.1 146.7 all-reduce.29
where the time goes:
time: 924 us; the launch traced here: 919 us
  waiting for transfers between devices  347 us (38%)
  matrix products  289 us (31%)
  blocking collectives  110 us (12%)
  other arithmetic  106 us (11%)
  local copies, waits for them, and re-layouts  36.5 us (4%)
  between operations  29.8 us (3%)
    dot_general x42, matrix products, product(): return jnp.dot(left, right, preferred_element_type=jnp.float32)  168 us
    reduce_scatter x1, waiting for transfers between devices, per_device(): lax.psum_scatter(pooled[1], 'shard', scatter_dimension=1, tiled=True)  130 us
    psum x1, waiting for transfers between devices, per_device(): pooled = lax.psum((full[0], full[1], full[2], full[3], full[4]), 'group')  129 us
    dot_general x2, matrix products, backward(): jnp.einsum('hqk,khd->qhd', d_scores, keys, preferred_element_type=jnp.flo...  41.9 us
    dot_general x2, matrix products, backward(): jnp.einsum('hqk,qhd->khd', d_scores, query, preferred_element_type=jnp.fl...  40.6 us
    psum x1, blocking collectives, per_device(): totals = lax.psum((local_count, local_loss), ('group', 'shard'))  39.7 us
    reduce_scatter x1, waiting for transfers between devices, per_device(): lax.psum_scatter(pooled[2], 'shard', scatter_dimension=0, tiled=True)  36.1 us
    reduce_scatter x1, waiting for transfers between devices, per_device(): lax.psum_scatter(pooled[4], 'shard', scatter_dimension=1, tiled=True)  35.4 us
  transfers between devices with their start and end apart: 8, of which 5 were waited for; matrix products, arithmetic and copies ran while one was open for 28% of the time, Pallas kernels for 0%

commit v1 on v0

v1 whole, which is shorter than its diff:
```python
import functools

import jax
import jax.numpy as jnp
from jax import lax
from jax.experimental import pallas as pl
from jax.experimental.pallas import tpu as pltpu
from jax.sharding import PartitionSpec as P

D = 768
CH = 512
HEADS = 12
HEAD_DIM = 64
FF = 3072
CD = 256
CODES = 500
CPAD = 512
LEN = 512
SPAN = 10
NVEC = 14

beta_one = 0.9
beta_two = 0.999
rate = 0.03
decay = 0.01
adam_eps = 1e-08
clip_norm = 0.01
temper = 10.0

F32 = jnp.float32
BF16 = jnp.bfloat16
VMEM_BYTES = 60 * 1024 * 1024


def product(left, right):
    return jnp.dot(left, right, preferred_element_type=F32)


def product_nt(left, right):
    return lax.dot_general(left, right, (((1,), (1,)), ((), ())), preferred_element_type=F32)


def product_tn(left, right):
    return lax.dot_general(left, right, (((0,), (0,)), ((), ())), preferred_element_type=F32)


def norm_parts(values):
    centred = values - jnp.mean(values, -1, keepdims=True)
    root = lax.rsqrt(jnp.mean(centred * centred, -1, keepdims=True) + 1e-05)
    return centred * root, root


def norm_back(upstream, hat, root, gain):
    scaled = upstream * gain
    return root * (
        scaled
        - jnp.mean(scaled, -1, keepdims=True)
        - hat * jnp.mean(scaled * hat, -1, keepdims=True)
    )


def column_sum(values):
    return jnp.sum(values, 0, keepdims=True)


def gelu_pair(e):
    root = 0.7071067811865476
    reach = jnp.abs(e) * root
    tail = jnp.exp(-0.5 * e * e)
    t = 1.0 / (1.0 + 0.3275911 * reach)
    poly = t * (
        0.254829592
        + t * (-0.284496736 + t * (1.421413741 + t * (-1.453152027 + t * 1.061405429)))
    )
    half = 0.5 * poly * tail
    phi = jnp.where(e < 0.0, half, 1.0 - half)
    return e * phi, phi + e * tail * 0.3989422804014327


def params(limit=VMEM_BYTES):
    return pltpu.CompilerParams(vmem_limit_bytes=limit)


def whole(shape):
    return pl.BlockSpec(shape, lambda *_: (0,) * len(shape), pipeline_mode=pl.Buffered(1))


def rows_of(tile, width):
    return pl.BlockSpec((tile, width), lambda i: (i, 0))


def project_kernel(x_ref, mask_ref, win_ref, w0_ref, vec_ref, a_ref, h_ref, hb_ref, t_ref):
    hat, _ = norm_parts(x_ref[...].astype(F32))
    normed = (hat * vec_ref[0:1, :CH].astype(F32) + vec_ref[1:2, :CH].astype(F32)).astype(BF16)
    a_ref[...] = normed
    hidden = product(normed, win_ref[...]) + vec_ref[2:3, :D].astype(F32)
    hidden = jnp.where(mask_ref[...] > 0.0, vec_ref[3:4, :D].astype(F32), hidden)
    h_ref[...] = hidden
    low = hidden.astype(BF16)
    hb_ref[...] = low
    t_ref[:, :D] = (
        product(low, w0_ref[:, :D]) + vec_ref[4:5, :D].astype(F32)
    ).astype(BF16)
    t_ref[:, D : 2 * D] = product(low, w0_ref[:, D : 2 * D]).astype(BF16)
    t_ref[:, 2 * D : 3 * D] = (
        product(low, w0_ref[:, 2 * D : 3 * D]) + vec_ref[5:6, :D].astype(F32)
    ).astype(BF16)


def project(x, masked, win, w0, vecs, tile):
    n = x.shape[0]
    return pl.pallas_call(
        project_kernel,
        grid=(n // tile,),
        in_specs=[
            rows_of(tile, CH),
            rows_of(tile, 1),
            whole((CH, D)),
            whole((D, FF)),
            whole((NVEC, FF)),
        ],
        out_specs=[rows_of(tile, CH), rows_of(tile, D), rows_of(tile, D), rows_of(tile, 3 * D)],
        out_shape=[
            jax.ShapeDtypeStruct((n, CH), BF16),
            jax.ShapeDtypeStruct((n, D), F32),
            jax.ShapeDtypeStruct((n, D), BF16),
            jax.ShapeDtypeStruct((n, 3 * D), BF16),
        ],
        compiler_params=params(),
        name="project",
    )(x, masked, win, w0, vecs)


def half_masks():
    lane = lax.broadcasted_iota(jnp.int32, (1, 128), 1)
    return [(lane < HEAD_DIM).astype(BF16), (lane >= HEAD_DIM).astype(BF16)]


def attend_kernel(len_ref, q_ref, k_ref, v_ref, o_ref):
    length = len_ref[pl.program_id(0)]
    shift = jnp.where(lax.broadcasted_iota(jnp.int32, (1, LEN), 1) < length, 0.0, -1e30)
    keys = k_ref[...]
    total = None
    for half in half_masks():
        scores = product_nt(q_ref[...] * half, keys) * HEAD_DIM ** (-0.5) + shift
        power = jnp.exp(scores - jnp.max(scores, -1, keepdims=True))
        probs = (power * (1.0 / jnp.sum(power, -1, keepdims=True))).astype(BF16)
        part = product(probs, v_ref[...] * half)
        total = part if total is None else total + part
    o_ref[...] = total.astype(BF16)


def attend(lengths, triple):
    n = triple.shape[0]
    pairs = D // 128
    return pl.pallas_call(
        attend_kernel,
        grid_spec=pltpu.PrefetchScalarGridSpec(
            num_scalar_prefetch=1,
            grid=(n // LEN, pairs),
            in_specs=[
                pl.BlockSpec((LEN, 128), lambda u, j, _: (u, j)),
                pl.BlockSpec((LEN, 128), lambda u, j, _: (u, pairs + j)),
                pl.BlockSpec((LEN, 128), lambda u, j, _: (u, 2 * pairs + j)),
            ],
            out_specs=pl.BlockSpec((LEN, 128), lambda u, j, _: (u, j)),
        ),
        out_shape=jax.ShapeDtypeStruct((n, D), BF16),
        compiler_params=params(),
        name="attend",
    )(lengths, triple, triple, triple)


def feed_kernel(
    scale_ref,
    att_ref,
    h_ref,
    mask_ref,
    label_ref,
    w0_ref,
    wu_ref,
    wd_ref,
    wh_ref,
    cu_ref,
    vec_ref,
    loss_ref,
    z1_ref,
    act_ref,
    de_ref,
    df_ref,
    z2_ref,
    dc_ref,
    dlog_ref,
    uc_ref,
    dr1_ref,
    dy_ref,
    do_ref,
    gv_ref,
    slope_ref,
):
    @pl.when(pl.program_id(0) == 0)
    def _():
        gv_ref[...] = jnp.zeros_like(gv_ref)
        loss_ref[...] = jnp.zeros_like(loss_ref)

    def vec(row, width=D):
        return vec_ref[row : row + 1, :width].astype(F32)

    masked = mask_ref[...]
    wo = w0_ref[:, 3 * D :]
    resid_one = h_ref[...] + product(att_ref[...], wo) + vec(6)
    hat_one, root_one = norm_parts(resid_one)
    first = hat_one * vec(7) + vec(8)
    first_low = first.astype(BF16)
    z1_ref[...] = first_low
    lowered = None
    for c in range(FF // D):
        cols = slice(c * D, (c + 1) * D)
        before = product(first_low, wu_ref[:, cols]) + vec_ref[9:10, cols].astype(F32)
        active, slope = gelu_pair(before)
        active = active.astype(BF16)
        act_ref[:, cols] = active
        slope_ref[:, cols] = slope
        part = product(active, wd_ref[cols, :])
        lowered = part if lowered is None else lowered + part
    resid_two = first + lowered + vec(10)
    hat_two, root_two = norm_parts(resid_two)
    second_low = (hat_two * vec(11) + vec(12)).astype(BF16)
    z2_ref[...] = second_low
    head = product(second_low, wh_ref[...]) + vec(13, CD)
    root_head = lax.rsqrt(jnp.sum(head * head, -1, keepdims=True) + 1e-06)
    unit = head * root_head
    unit_low = unit.astype(BF16)
    uc_ref[...] = unit_low
    logits = temper * product_nt(unit_low, cu_ref[...])
    code = lax.broadcasted_iota(jnp.int32, logits.shape, 1)
    logits = jnp.where(code < CODES, logits, -1e30)
    top = jnp.max(logits, -1, keepdims=True)
    power = jnp.exp(logits - top)
    total = jnp.sum(power, -1, keepdims=True)
    onehot = code == label_ref[...]
    picked = jnp.sum(jnp.where(onehot, logits, 0.0), -1, keepdims=True)
    losses = top + jnp.log(total) - picked
    loss_ref[...] += jnp.sum(jnp.where(masked > 0.0, losses, 0.0), 0, keepdims=True)
    chances = power * (1.0 / total)
    d_logit = (
        temper
        * (
            jnp.where(masked > 0.0, chances - jnp.where(onehot, 1.0, 0.0), 0.0)
            * scale_ref[0]
        )
    ).astype(BF16)
    dlog_ref[...] = d_logit
    d_unit = product(d_logit, cu_ref[...])
    d_head = (root_head * (d_unit - unit * jnp.sum(d_unit * unit, -1, keepdims=True))).astype(BF16)
    dc_ref[...] = d_head
    gv_ref[13:14, :CD] += column_sum(d_head.astype(F32))
    d_second = product_nt(d_head, wh_ref[...])
    gv_ref[11:12, :D] += column_sum(d_second * hat_two)
    gv_ref[12:13, :D] += column_sum(d_second)
    d_resid_two = norm_back(d_second, hat_two, root_two, vec(11))
    d_lower = d_resid_two.astype(BF16)
    df_ref[...] = d_lower
    gv_ref[10:11, :D] += column_sum(d_lower.astype(F32))
    d_first = d_resid_two
    for c in range(FF // D):
        cols = slice(c * D, (c + 1) * D)
        d_before = (slope_ref[:, cols] * product_nt(d_lower, wd_ref[cols, :])).astype(BF16)
        de_ref[:, cols] = d_before
        gv_ref[9:10, cols] += column_sum(d_before.astype(F32))
        d_first = d_first + product_nt(d_before, wu_ref[:, cols])
    gv_ref[7:8, :D] += column_sum(d_first * hat_one)
    gv_ref[8:9, :D] += column_sum(d_first)
    d_resid_one = norm_back(d_first, hat_one, root_one, vec(7))
    dr1_ref[...] = d_resid_one
    d_branch = d_resid_one.astype(BF16)
    dy_ref[...] = d_branch
    gv_ref[6:7, :D] += column_sum(d_branch.astype(F32))
    do_ref[...] = product_nt(d_branch, wo).astype(BF16)


def feed(scale, att, hidden, masked, label, w0, wu, wd, wh, cu, vecs, tile):
    n = att.shape[0]
    outs = [
        (D, BF16),
        (FF, BF16),
        (FF, BF16),
        (D, BF16),
        (D, BF16),
        (CD, BF16),
        (CPAD, BF16),
        (CD, BF16),
        (D, F32),
        (D, BF16),
        (D, BF16),
    ]
    return pl.pallas_call(
        feed_kernel,
        grid=(n // tile,),
        in_specs=[
            pl.BlockSpec(memory_space=pltpu.SMEM),
            rows_of(tile, D),
            rows_of(tile, D),
            rows_of(tile, 1),
            rows_of(tile, 1),
            whole((D, FF)),
            whole((D, FF)),
            whole((FF, D)),
            whole((D, CD)),
            whole((CPAD, CD)),
            whole((NVEC, FF)),
        ],
        out_specs=[pl.BlockSpec((1, 1), lambda i: (0, 0))]
        + [rows_of(tile, width) for width, _ in outs]
        + [pl.BlockSpec((16, FF), lambda i: (0, 0))],
        out_shape=[jax.ShapeDtypeStruct((1, 1), F32)]
        + [jax.ShapeDtypeStruct((n, width), kind) for width, kind in outs]
        + [jax.ShapeDtypeStruct((16, FF), F32)],
        scratch_shapes=[pltpu.VMEM((tile, FF), F32)],
        compiler_params=params(),
        name="feed",
    )(scale, att, hidden, masked, label, w0, wu, wd, wh, cu, vecs)


def attend_back_kernel(len_ref, q_ref, k_ref, v_ref, do_ref, dq_ref, dk_ref, dv_ref):
    length = len_ref[pl.program_id(0)]
    shift = jnp.where(lax.broadcasted_iota(jnp.int32, (LEN, 1), 0) < length, 0.0, -1e30)
    keys, values = k_ref[...], v_ref[...]
    dq = dk = dv = None
    for half in half_masks():
        query = q_ref[...] * half
        upstream = do_ref[...] * half
        scores = product_nt(keys, query) * HEAD_DIM ** (-0.5) + shift
        power = jnp.exp(scores - jnp.max(scores, 0, keepdims=True))
        probs = power * (1.0 / jnp.sum(power, 0, keepdims=True))
        part_v = product(probs.astype(BF16), upstream)
        d_probs = product_nt(values, upstream)
        weight = jnp.sum(probs * d_probs, 0, keepdims=True)
        d_scores = (probs * (d_probs - weight) * HEAD_DIM ** (-0.5)).astype(BF16)
        part_k = product(d_scores, query)
        part_q = product_tn(d_scores, keys * half)
        dq = part_q if dq is None else dq + part_q
        dk = part_k if dk is None else dk + part_k
        dv = part_v if dv is None else dv + part_v
    dq_ref[...] = dq.astype(BF16)
    dk_ref[...] = dk.astype(BF16)
    dv_ref[...] = dv.astype(BF16)


def attend_back(lengths, triple, d_att):
    n = triple.shape[0]
    pairs = D // 128
    block = pl.BlockSpec((LEN, 128), lambda u, j, _: (u, j))
    return pl.pallas_call(
        attend_back_kernel,
        grid_spec=pltpu.PrefetchScalarGridSpec(
            num_scalar_prefetch=1,
            grid=(n // LEN, pairs),
            in_specs=[
                block,
                pl.BlockSpec((LEN, 128), lambda u, j, _: (u, pairs + j)),
                pl.BlockSpec((LEN, 128), lambda u, j, _: (u, 2 * pairs + j)),
                block,
            ],
            out_specs=[block] * 3,
        ),
        out_shape=[jax.ShapeDtypeStruct((n, D), BF16)] * 3,
        compiler_params=params(),
        name="attend_back",
    )(lengths, triple, triple, triple, d_att)


def project_back_kernel(
    dq_ref, dk_ref, dv_ref, dr1_ref, mask_ref, x_ref, win_ref, w0_ref, gvin_ref, dhh_ref, gv_ref
):
    @pl.when(pl.program_id(0) == 0)
    def _():
        gv_ref[...] = gvin_ref[...]

    dq, dk, dv = dq_ref[...], dk_ref[...], dv_ref[...]
    gv_ref[4:5, :D] += column_sum(dq.astype(F32))
    gv_ref[5:6, :D] += column_sum(dv.astype(F32))
    d_hidden = (
        dr1_ref[...]
        + product_nt(dq, w0_ref[:, :D])
        + product_nt(dk, w0_ref[:, D : 2 * D])
        + product_nt(dv, w0_ref[:, 2 * D : 3 * D])
    )
    masked = mask_ref[...] > 0.0
    gv_ref[3:4, :D] += column_sum(jnp.where(masked, d_hidden, 0.0))
    d_proj = jnp.where(masked, 0.0, d_hidden).astype(BF16)
    dhh_ref[...] = d_proj
    gv_ref[2:3, :D] += column_sum(d_proj.astype(F32))
    d_normed = product_nt(d_proj, win_ref[...])
    hat, _ = norm_parts(x_ref[...].astype(F32))
    gv_ref[0:1, :CH] += column_sum(d_normed * hat)
    gv_ref[1:2, :CH] += column_sum(d_normed)


def project_back(dq, dk, dv, dr1, masked, x, win, w0, gv, tile):
    n = x.shape[0]
    return pl.pallas_call(
        project_back_kernel,
        grid=(n // tile,),
        in_specs=[
            rows_of(tile, D),
            rows_of(tile, D),
            rows_of(tile, D),
            rows_of(tile, D),
            rows_of(tile, 1),
            rows_of(tile, CH),
            whole((CH, D)),
            whole((D, FF)),
            whole((16, FF)),
        ],
        out_specs=[rows_of(tile, D), pl.BlockSpec((16, FF), lambda i: (0, 0))],
        out_shape=[
            jax.ShapeDtypeStruct((n, D), BF16),
            jax.ShapeDtypeStruct((16, FF), F32),
        ],
        compiler_params=params(),
        name="project_back",
    )(dq, dk, dv, dr1, masked, x, win, w0, gv)


def unit_rows(values):
    return values * lax.rsqrt(jnp.sum(values * values, -1, keepdims=True) + 1e-06)


def span_mask(length, begins):
    position = jnp.arange(LEN, dtype=jnp.int32)
    first = begins % (length - SPAN + 1)
    inside = (position[None, :] >= first[:, None]) & (position[None, :] < first[:, None] + SPAN)
    return jnp.any(inside, 0) & (position < length)


def per_device(
    features,
    lengths,
    starts,
    labels,
    step_count,
    weight_in,
    weight_rows,
    weight_down,
    weight_head,
    vectors,
    moment_in,
    moment_rows,
    moment_down,
    moment_head,
    moment_vectors,
    second_in,
    second_rows,
    second_down,
    second_head,
    second_vectors,
):
    masters = (weight_in, weight_rows, weight_down, weight_head, vectors)
    moments = (moment_in, moment_rows, moment_down, moment_head, moment_vectors)
    seconds = (second_in, second_rows, second_down, second_head, second_vectors)
    utters = features.shape[0]
    n = utters * LEN
    masked = jax.vmap(span_mask)(lengths, starts)
    count = lax.psum(jnp.sum(masked.astype(F32)), ("group", "shard"))
    scale = jnp.reshape(1.0 / count, (1,))
    masked = masked.astype(F32).reshape(n, 1)
    label = labels.reshape(n, 1)
    x = features.reshape(n, CH)
    low = tuple(w.astype(BF16) for w in masters)
    win = lax.all_gather(low[0], "shard", axis=0, tiled=True)
    vecs = lax.all_gather(low[4], "shard", axis=1, tiled=True)
    w0 = lax.all_gather(low[1][0], "shard", axis=0, tiled=True)
    wu = lax.all_gather(low[1][1], "shard", axis=0, tiled=True)
    wd = lax.all_gather(low[2], "shard", axis=0, tiled=True)
    whead = lax.all_gather(low[3], "shard", axis=1, tiled=True)
    wh = whead[:D]
    codes = jnp.pad(whead[D:].astype(F32), ((0, CPAD - CODES), (0, 0)))
    cu = unit_rows(codes).astype(BF16)

    a, hidden, hid_low, triple = project(x, masked, win, w0, vecs, 256)
    att = attend(lengths, triple)
    loss, z1, act, de, df, z2, dc, dlog, uc, dr1, dy, d_att, gv = feed(
        scale, att, hidden, masked, label, w0, wu, wd, wh, cu, vecs, 256
    )
    g_lower = product_tn(act, df)
    g_up = product_tn(z1, de)
    g_final = product_tn(z2, dc)
    d_codes_unit = product_tn(dlog, uc)
    _, codes_back = jax.vjp(unit_rows, codes)
    g_codes = codes_back(d_codes_unit)[0][:CODES]
    dq, dk, dv = attend_back(lengths, triple, d_att)
    dhh, gv = project_back(dq, dk, dv, dr1, masked, x, win, w0, gv, 256)
    g_block = jnp.concatenate(
        [
            product_tn(hid_low, dq),
            product_tn(hid_low, dk),
            product_tn(hid_low, dv),
            product_tn(att, dy),
        ],
        1,
    )
    g_input = product_tn(a, dhh)
    scattered = (
        lax.psum_scatter(g_input, "shard", scatter_dimension=0, tiled=True),
        jnp.stack(
            [
                lax.psum_scatter(g_block, "shard", scatter_dimension=0, tiled=True),
                lax.psum_scatter(g_up, "shard", scatter_dimension=0, tiled=True),
            ]
        ),
        lax.psum_scatter(g_lower, "shard", scatter_dimension=0, tiled=True),
        lax.psum_scatter(
            jnp.concatenate([g_final, g_codes], 0), "shard", scatter_dimension=1, tiled=True
        ),
        lax.psum_scatter(gv[:NVEC], "shard", scatter_dimension=1, tiled=True),
    )
    summed = lax.psum(scattered, "group")
    loss = lax.psum(loss[0, 0], ("group", "shard")) / count
    local_squares = sum((jnp.sum(g * g) for g in summed))
    norm = jnp.sqrt(lax.psum(local_squares, "shard"))
    factor = jnp.minimum(1.0, clip_norm / (norm + 1e-06))
    steps = step_count[0].astype(F32)
    fix_one = 1.0 - jnp.power(beta_one, steps)
    fix_two = 1.0 - jnp.power(beta_two, steps)
    decays = (decay, decay, decay, decay, 0.0)
    new_w, new_m, new_v = ([], [], [])
    for weight, grad, moment, square, shrink in zip(masters, summed, moments, seconds, decays):
        grad = grad * factor
        moment = beta_one * moment + (1.0 - beta_one) * grad
        square = beta_two * square + (1.0 - beta_two) * grad * grad
        stepped = moment / fix_one / (jnp.sqrt(square / fix_two) + adam_eps)
        new_w.append(weight - rate * (stepped + shrink * weight))
        new_m.append(moment)
        new_v.append(square)
    copies = [w.astype(BF16) for w in new_w]
    return (
        *new_w,
        *new_m,
        *new_v,
        *copies,
        jnp.reshape(loss, (1,)),
        jnp.reshape(norm, (1,)),
    )


def solution(mesh):
    weights = (
        P("shard", None),
        P(None, "shard", None),
        P("shard", None),
        P(None, "shard"),
        P(None, "shard"),
    )
    both = ("group", "shard")
    in_specs = (P(both, None, None), P(both), P(both, None), P(both, None), P()) + weights * 3
    out_specs = weights * 4 + (P(), P())
    return jax.shard_map(
        per_device, mesh=mesh, in_specs=in_specs, out_specs=out_specs, check_vma=False
    )
```

time: 924 us -> 802 us (0.87)
  matrix products: 289 us -> 33.5 us
  Pallas kernels: 0 us -> 124 us
  other arithmetic: 106 us -> 31.3 us
  waiting for transfers between devices: 347 us -> 410 us
  blocking collectives: 110 us -> 152 us
  local copies, waits for them, and re-layouts: 36.5 us -> 21 us
    dot_general x54 -> x8, matrix products: 289 us -> 23 us  [product_tn(): lax.dot_general(left, right, (((0,), (0,)), ((), ())), preferred_element_...]
    pallas_call x0 -> x5, Pallas kernels: none -> 124 us  [the longest x1 49.1 us: feed(): pl.pallas_call(feed_kernel, grid=(n // tile,), in_specs=[pl.BlockSpec(mem...]
    psum x2 -> x3, blocking collectives: 59.9 us -> 102 us  [the longest x1 42.4 us: per_device(): count = lax.psum(jnp.sum(masked.astype(F32)), ('group', 'shard'))]
    unnamed x9 -> x11, waiting for transfers between devices: 0.15 us -> 39.3 us
    reduce_scatter x4 -> x5, waiting for transfers between devices: 201 us -> 234 us  [the longest x1 80 us: per_device(): lax.psum_scatter(g_lower, 'shard', scatter_dimension=0, tiled=True)]
    convert_element_type x16 -> x11, other arithmetic: 41.4 us -> 16.8 us  [the longest x5 13.2 us: per_device(): copies = [w.astype(BF16) for w in new_w]]
    reduce_sum x22 -> x1, other arithmetic: 21.9 us -> 0.68 us  [per_device(): count = lax.psum(jnp.sum(masked.astype(F32)), ('group', 'shard'))]
    another operation x2 -> x1, other arithmetic: 16.4 us -> 3.26 us  [per_device(): jnp.stack([lax.psum_scatter(g_block, 'shard', scatter_dimension=0, tiled=...]
  transfers between devices with their start and end apart: 8 -> 10, of which waited for: 5 -> 7; matrix products, arithmetic and copies ran while one was open for 28% -> 5% of each run, Pallas kernels for 0% -> 5%
where the time goes in v1:
time: 802 us; the launch traced here: 796 us
  waiting for transfers between devices  410 us (51%)
  blocking collectives  152 us (19%)
  Pallas kernels  124 us (15%)
  matrix products  33.5 us (4%)
  other arithmetic  31.3 us (4%)
  between operations  24 us (3%)
  local copies, waits for them, and re-layouts  21 us (3%)
    psum x1, waiting for transfers between devices, per_device(): summed = lax.psum(scattered, 'group')  126 us
    reduce_scatter x1, waiting for transfers between devices, per_device(): lax.psum_scatter(g_lower, 'shard', scatter_dimension=0, tiled=True)  80 us
    reduce_scatter x1, waiting for transfers between devices, per_device(): lax.psum_scatter(g_up, 'shard', scatter_dimension=0, tiled=True)  79.9 us
    pallas_call x1, Pallas kernels, feed(): pl.pallas_call(feed_kernel, grid=(n // tile,), in_specs=[pl.BlockSpec(mem...  49.1 us
    psum x1, blocking collectives, per_device(): count = lax.psum(jnp.sum(masked.astype(F32)), ('group', 'shard'))  42.4 us
    reduce_scatter x1, waiting for transfers between devices, per_device(): lax.psum_scatter(g_input, 'shard', scatter_dimension=0, tiled=True)  42.4 us
    psum x1, blocking collectives, per_device(): loss = lax.psum(loss[0, 0], ('group', 'shard')) / count  39.6 us
    unnamed x11, waiting for transfers between devices  39.3 us
  transfers between devices with their start and end apart: 10, of which 7 were waited for; matrix products, arithmetic and copies ran while one was open for 5% of the time, Pallas kernels for 5%

profile of v1, /device:TPU:0, one launch (start us, length us, event | category | flops | bytes accessed | tf_op | source)
XLA Modules:
  0.0 795.9 jit_solution(8373916116227104668)
XLA Ops:
  13.0 42.4 %psum.56 = f32[]{:T(128)} all-reduce(f32[]{:T(128)} %fusion.7), channel_id=1, replica_groups=mesh['group'=4,'shard'=8] {'group','shard'}, use_global_device_ids=true, to_apply=%region_2.3 | all-reduce | flops 1 | bytes 8 | tf_op jit(solution)/shard_map/psum | solution.py:465
  55.5 11.7 %all_gather.23 = bf16[1268,256]{0,1:T(8,128)(2,1)S(1)} all-gather(bf16[1268,32]{0,1:T(8,128)(2,1)S(1)} %convert_element_type.63), channel_id=1, replica_groups=mesh['group'=4,'shard'=8] {'shard'}, dimensions={1}, use_global_device_ids=true | all-gather | bytes 730368 | tf_op jit(solution)/shard_map/all_gather | solution.py:476
  71.4 9.7 %all_gather.20.vec_ref = bf16[14,3072]{1,0:T(8,128)(2,1)} all-gather(bf16[14,384]{1,0:T(8,128)(2,1)S(1)} %convert_element_type.60), channel_id=1, replica_groups=mesh['group'=4,'shard'=8] {'shard'}, dimensions={1}, use_global_device_ids=true | all-gather | bytes 96768 | tf_op jit(solution)/shard_map/all_gather | solution.py:472
  81.1 14.9 %all_gather.18.win_ref = bf16[512,768]{1,0:T(8,128)(2,1)} all-gather(bf16[64,768]{1,0:T(8,128)(2,1)S(1)} %convert_element_type.58), channel_id=1, replica_groups=mesh['group'=4,'shard'=8] {'shard'}, dimensions={0}, use_global_device_ids=true | all-gather | bytes 884736 | tf_op jit(solution)/shard_map/all_gather | solution.py:471
  96.8 10.4 %project.1 = (bf16[1024,512]{1,0:T(8,128)(2,1)}, f32[1024,768]{1,0:T(8,128)}, bf16[1024,768]{1,0:T(8,128)(2,1)}, bf16[1024,2304]{1,0:T(8,128)(2,1)}) custom-call(bf16[1024,512]{1,0:T(8,128)(2,1)} %bitcast.53, f32[1024,1]{1,0:T(8,128)} %bitcast.48, bf16[512,768]{1,0:T(8,128)(2,1)} %all_gather.18.win_ref, bf16[768,3072]{1,0:T(8,128)(2,1)} %bitcast.45, ...), custom_call_target="tpu_custom_call" | custom-call | tf_op jit(solution)/shard_map/project/pallas_call | solution.py:112
  107.2 21.3 %attend.1.att_ref = bf16[1024,768]{1,0:T(8,128)(2,1)} custom-call(s32[2]{0:T(128)} %len_ref.3, bf16[1024,2304]{1,0:T(8,128)(2,1)} %get-tuple-element.45.q_ref.k_ref.v_ref, bf16[1024,2304]{1,0:T(8,128)(2,1)} %get-tuple-element.45.q_ref.k_ref.v_ref, bf16[1024,2304]{1,0:T(8,128)(2,1)} %get-tuple-element.45.q_ref.k_ref.v_ref), custom_call_target="tpu_custom_call" | custom-call | tf_op jit(solution)/shard_map/attend/pallas_call | solution.py:156
  128.5 10.1 %all-gather.6.cloned.1.call-done.wd_ref = bf16[3072,768]{1,0:T(8,128)(2,1)} async-done(((bf16[384,768]{1,0:T(8,128)(2,1)}), bf16[3072,768]{1,0:T(8,128)(2,1)}) %all-gather.6.cloned.1.call-update) | async-done | bytes 4718608 | tf_op jit(solution)/shard_map/all_gather | solution.py:475
  138.7 49.1 %feed.1 = (f32[1,1]{1,0:T(1,128)}, bf16[1024,768]{1,0:T(8,128)(2,1)}, bf16[1024,3072]{1,0:T(8,128)(2,1)}, bf16[1024,3072]{1,0:T(8,128)(2,1)}, bf16[1024,768]{1,0...) custom-call(f32[1]{0:T(128)} %bitcast.2.scale_ref, ...), custom_call_target="tpu_custom_call" | custom-call | tf_op jit(solution)/shard_map/feed/pallas_call | solution.py:297
  187.7 31.1 %attend_back.1 = (bf16[1024,768]{1,0:T(8,128)(2,1)}, bf16[1024,768]{1,0:T(8,128)(2,1)}, bf16[1024,768]{1,0:T(8,128)(2,1)}) custom-call(s32[2]{0:T(128)} %len_ref.3, bf16[1024,2304]{1,0:T(8,128)(2,1)} %get-tuple-element.45.q_ref.k_ref.v_ref, bf16[1024,2304]{1,0:T(8,128)(2,1)} %get-tuple-element.45.q_ref.k_ref.v_ref, ...), custom_call_target="tpu_custom_call" | custom-call | tf_op jit(solution)/shard_map/attend_back/pallas_call | solution.py:354
  231.2 9.7 %copy.139 = f32[768,3072]{1,0:T(8,128)} copy(f32[768,3072]{0,1:T(8,128)} %pad_maximum_fusion) | data formatting | bytes 18874368
  240.9 10.5 %fusion.25 = f32[768,3072]{1,0:T(8,128)} fusion(bf16[1024,768]{1,0:T(8,128)(2,1)} %get-tuple-element.56, bf16[1024,3072]{1,0:T(8,128)(2,1)} %get-tuple-element.57), kind=kOutput, calls=%fused_computation.59 | convolution fusion | flops 4831838208 | bytes 17301504
  257.3 11.9 %project_back.1 = (bf16[1024,768]{1,0:T(8,128)(2,1)}, f32[16,3072]{1,0:T(8,128)}) custom-call(bf16[1024,768]{1,0:T(8,128)(2,1)} %get-tuple-element.48.dq_ref, bf16[1024,768]{1,0:T(8,128)(2,1)} %get-tuple-element.49.dk_ref, bf16[1024,768]{1,0:T(8,128)(2,1)} %get-tuple-element.50.dv_ref, f32[1024,768]{1,0:T(8,128)} %get-tuple-element.51.dr1_ref, ...), custom_call_target="tpu_custom_call" | custom-call | tf_op jit(solution)/shard_map/project_back/pallas_call | solution.py:402
  274.4 10.2 %fusion.26 = f32[3072,768]{1,0:T(8,128)} fusion(bf16[1024,3072]{1,0:T(8,128)(2,1)} %get-tuple-element.58, bf16[1024,768]{1,0:T(8,128)(2,1)S(1)} %copy-done.23), kind=kOutput, calls=%fused_computation.60 | convolution fusion | flops 4831838208 | bytes 17301504 | tf_op jit(solution)/shard_map/dot_general | solution.py:44
  285.4 32.1 %reduce-scatter.19.cloned.1.call-done = f32[96,3072]{1,0:T(8,128)} async-done(((f32[768,3072]{1,0:T(8,128)}), f32[96,3072]{1,0:T(8,128)}) %reduce-scatter.19.cloned.1.call-update) | async-done | bytes 1179664 | tf_op jit(solution)/shard_map/reduce_scatter | solution.py:508
  317.5 79.9 %reduce-scatter.21.cloned.1.call-done = f32[96,3072]{1,0:T(8,128)} async-done(((f32[768,3072]{1,0:T(8,128)}), f32[96,3072]{1,0:T(8,128)}) %reduce-scatter.21.cloned.1.call-update) | async-done | bytes 1179664 | tf_op jit(solution)/shard_map/reduce_scatter | solution.py:509
  400.7 37.8 %reduce-scatter.23.cloned.1.call-done = f32[32,1268]{1,0:T(8,128)} async-done(((f32[256,1268]{1,0:T(8,128)}), f32[32,1268]{1,0:T(8,128)}) %reduce-scatter.23.cloned.1.call-update) | async-done | bytes 162320
  438.4 42.4 %reduce-scatter.13.cloned.1.call-done = f32[64,768]{1,0:T(8,128)} async-done(((f32[512,768]{1,0:T(8,128)}), f32[64,768]{1,0:T(8,128)}) %reduce-scatter.13.cloned.1.call-update) | async-done | bytes 196624 | tf_op jit(solution)/shard_map/reduce_scatter | solution.py:505
  480.8 80.0 %reduce-scatter.15.cloned.1.call-done = f32[384,768]{1,0:T(8,128)} async-done(((f32[3072,768]{1,0:T(8,128)}), f32[384,768]{1,0:T(8,128)}) %reduce-scatter.15.cloned.1.call-update) | async-done | bytes 1179664 | tf_op jit(solution)/shard_map/reduce_scatter | solution.py:512
  561.6 39.6 %psum.63 = f32[]{:T(128)} all-reduce(f32[]{:T(128)} %bitcast.8), channel_id=1, replica_groups=mesh['group'=4,'shard'=8] {'group','shard'}, use_global_device_ids=true, to_apply=%region_22.23 | all-reduce | flops 1 | bytes 8 | tf_op jit(solution)/shard_map/psum | solution.py:519
  601.2 19.8 %psum.61 = f32[14,384]{1,0:T(8,128)S(1)} all-reduce(f32[14,384]{1,0:T(8,128)} %reduce-scatter.17.cloned.1.call-done), channel_id=1, replica_groups=mesh['group'=4,'shard'=8] {'group'}, use_global_device_ids=true, to_apply=%region_19.20 | all-reduce | flops 5376 | bytes 43008 | tf_op jit(solution)/shard_map/psum | solution.py:518
  621.6 125.9 %all-reduce.4.cloned.1.call-done = (f32[64,768]{1,0:T(8,128)}, f32[2,96,3072]{2,1,0:T(8,128)}, f32[384,768]{1,0:T(8,128)}, f32[1268,32]{0,1:T(8,128)}) async-done(((f32[64,768]{1,0:T(8,128)}, f32[2,96,3072]{2,1,0:T(8,128)}, f32[384,768]{1,0:T(8,128)}, f32[1268,32]{0,1:T(8,128)}), (f32[64,768]{1,0:T(8,128)}, f32[2,96,3072]{2,1,0:T(8,128)}, f32[384,768]{1,0:T(8,128)}, ...) | async-done | bytes 3897872 | tf_op jit(solution)/shard_map/psum | solution.py:518
  757.3 14.2 %psum.62 = f32[]{:T(128)} all-reduce(f32[]{:T(128)S(6)} %add.165), channel_id=1, replica_groups=mesh['group'=4,'shard'=8] {'shard'}, use_global_device_ids=true, to_apply=%region_21.22 | all-reduce | flops 1 | bytes 8 | tf_op jit(solution)/shard_map/psum | solution.py:521
  775.8 4.0 fusion.13
  780.7 4.7 fusion.15
  (130 shorter events, 48.8 us)
Async XLA Ops:
  7.2 89.6 %all-gather.8.cloned.1.call-start = ((), (), s32[]{:S(2)}) async-start(), calls=%async_computation.10 | async-start | bytes 5308416 | tf_op jit(solution)/shard_map/all_gather | solution.py:473
  10.2 45.2 %copy-start.15 = (f32[1268,32]{0,1:T(8,128)S(1)}, f32[1268,32]{0,1:T(8,128)}, u32[]{:S(2)}) copy-start(f32[1268,32]{0,1:T(8,128)} %param.28) | copy-start | bytes 486916
  10.2 118.3 %all-gather.10.cloned.1.call-start = ((), (), s32[]{:S(2)}) async-start(), calls=%async_computation.11 | async-start | bytes 5308416 | tf_op jit(solution)/shard_map/all_gather | solution.py:474
  11.0 127.7 %all-gather.6.cloned.1.call-start = ((), (), s32[]{:S(2)}) async-start(), calls=%async_computation.6 | async-start | bytes 5308416 | tf_op jit(solution)/shard_map/all_gather | solution.py:475
  11.9 56.4 %copy-start.10 = (f32[64,768]{1,0:T(8,128)S(1)}, f32[64,768]{1,0:T(8,128)}, u32[]{:S(2)}) copy-start(f32[64,768]{1,0:T(8,128)} %param.25) | copy-start | bytes 589828
  11.9 305.6 %reduce-scatter.19.cloned.1.call-start = ((), (), s32[]{:S(2)}) async-start(), calls=%async_computation.12 | async-start | bytes 10616832 | tf_op jit(solution)/shard_map/reduce_scatter | solution.py:508
  12.2 56.2 %copy-start.19 = (f32[14,384]{1,0:T(8,128)S(1)}, f32[14,384]{1,0:T(8,128)}, u32[]{:S(2)}) copy-start(f32[14,384]{1,0:T(8,128)} %param.29) | copy-start | bytes 64516
  240.9 156.5 %reduce-scatter.21.cloned.1.call-start = ((), (), s32[]{:S(2)}) async-start(), calls=%async_computation.13 | async-start | bytes 10616832 | tf_op jit(solution)/shard_map/reduce_scatter | solution.py:509
  251.4 187.0 %reduce-scatter.23.cloned.1.call-start = ((), (), s32[]{:S(2)}) async-start(), calls=%async_computation.14 | async-start | bytes 1474560
  257.3 223.6 %reduce-scatter.13.cloned.1.call-start = ((), (), s32[]{:S(2)}) async-start(), calls=%async_computation.7 | async-start | bytes 1769472 | tf_op jit(solution)/shard_map/reduce_scatter | solution.py:505
  257.3 12.0 %copy-start.27 = (bf16[1024,512]{1,0:T(8,128)(2,1)S(1)}, bf16[1024,512]{1,0:T(8,128)(2,1)}, u32[]{:S(2)}) copy-start(bf16[1024,512]{1,0:T(8,128)(2,1)} %get-tuple-element.44) | copy-start | bytes 3145732
  272.9 287.9 %reduce-scatter.15.cloned.1.call-start = ((), (), s32[]{:S(2)}) async-start(), calls=%async_computation.8 | async-start | bytes 10616832 | tf_op jit(solution)/shard_map/reduce_scatter | solution.py:512
  284.7 316.5 %reduce-scatter.17.cloned.1.call-start = ((), (), s32[]{:S(2)}) async-start(), calls=%async_computation.9 | async-start | bytes 221184 | tf_op jit(solution)/shard_map/reduce_scatter | solution.py:516
  285.4 462.1 %all-reduce.4.cloned.1.call-start = ((), (), s32[]{:S(2)}) async-start(), calls=%async_computation.15 | async-start | bytes 7798784 | tf_op jit(solution)/shard_map/psum | solution.py:518
  747.5 4.6 copy-start.14
  750.5 25.3 %copy-start.9 = (f32[384,768]{1,0:T(8,128)S(1)}, f32[384,768]{1,0:T(8,128)}, u32[]{:S(2)}) copy-start(f32[384,768]{1,0:T(8,128)} %param.37) | copy-start | bytes 3538948
  773.6 6.2 copy-start.6
  775.8 4.0 copy-start
  775.8 4.0 copy-start.1
  775.8 4.9 copy-start.5
  780.7 4.7 copy-start.11
  780.7 4.7 copy-start.13
  780.7 4.7 copy-start.17
  780.7 4.7 copy-start.18
  (17 other events, 35.6 us)
Sparse Core Ops, SparseCore 0:
  10.5 42.1 all-gather.7
  55.1 42.1 all-gather.9
  99.7 38.8 all-gather.5
  241.0 76.4 reduce-scatter.18
  320.9 76.4 reduce-scatter.20
  401.1 37.3 reduce-scatter.22
  442.3 38.4 reduce-scatter.12
  484.3 76.4 reduce-scatter.14
  564.5 32.6 reduce-scatter.16
  600.2 147.2 all-reduce.3

commit v2 on v1

--- a/solution.py
+++ b/solution.py
@@ -227,12 +227,12 @@
     hat_two, root_two = norm_parts(resid_two)
     second_low = (hat_two * vec(11) + vec(12)).astype(BF16)
     z2_ref[...] = second_low
-    head = product(second_low, wh_ref[...]) + vec(13, CD)
+    head = product_nt(second_low, wh_ref[...]) + vec(13, CD)
     root_head = lax.rsqrt(jnp.sum(head * head, -1, keepdims=True) + 1e-06)
     unit = head * root_head
     unit_low = unit.astype(BF16)
     uc_ref[...] = unit_low
-    logits = temper * product_nt(unit_low, cu_ref[...])
+    logits = temper * product(unit_low, cu_ref[...])
     code = lax.broadcasted_iota(jnp.int32, logits.shape, 1)
     logits = jnp.where(code < CODES, logits, -1e30)
     top = jnp.max(logits, -1, keepdims=True)
@@ -251,11 +251,11 @@
         )
     ).astype(BF16)
     dlog_ref[...] = d_logit
-    d_unit = product(d_logit, cu_ref[...])
+    d_unit = product_nt(d_logit, cu_ref[...])
     d_head = (root_head * (d_unit - unit * jnp.sum(d_unit * unit, -1, keepdims=True))).astype(BF16)
     dc_ref[...] = d_head
     gv_ref[13:14, :CD] += column_sum(d_head.astype(F32))
-    d_second = product_nt(d_head, wh_ref[...])
+    d_second = product(d_head, wh_ref[...])
     gv_ref[11:12, :D] += column_sum(d_second * hat_two)
     gv_ref[12:13, :D] += column_sum(d_second)
     d_resid_two = norm_back(d_second, hat_two, root_two, vec(11))
@@ -306,8 +306,8 @@
             whole((D, FF)),
             whole((D, FF)),
             whole((FF, D)),
-            whole((D, CD)),
-            whole((CPAD, CD)),
+            whole((CD, D)),
+            whole((CD, CPAD)),
             whole((NVEC, FF)),
         ],
         out_specs=[pl.BlockSpec((1, 1), lambda i: (0, 0))]
@@ -423,8 +423,432 @@
     )(dq, dk, dv, dr1, masked, x, win, w0, gv)
 
 
-def unit_rows(values):
-    return values * lax.rsqrt(jnp.sum(values * values, -1, keepdims=True) + 1e-06)
+MESH = pl.DeviceIdType.MESH
+
+
+def ceil_to(value, step):
+    return -(-value // step) * step
+
+
+class Chunk:
+    def __init__(self, names, rows, group, wide_xy, wide_z):
+        self.names = names
+        self.used = sum(rows)
+        self.starts = [sum(rows[:i]) for i in range(len(rows))]
+        self.piece_rows = rows
+        self.rows = ceil_to(self.used, 16 * group)
+        self.part = self.rows // group
+        self.kind_xy = F32 if wide_xy else BF16
+        self.kind_z = F32 if wide_z else BF16
+
+
+def tiles(rows, step, body):
+    def once(i, carry):
+        body(pl.ds(pl.multiple_of(i * step, step), step))
+        return carry
+
+    lax.fori_loop(0, rows // step, once, 0)
+
+
+def reduce_kernel(chunks, groups, shards, *refs):
+    chips = shards // 2
+    n = len(chunks)
+    refs = list(refs)
+
+    def take(count):
+        out = refs[:count]
+        del refs[:count]
+        return out
+
+    pieces = [take(len(c.names)) for c in chunks]
+    (loss_ref,) = take(1)
+    outs = take(n)
+    (stat_ref,) = take(1)
+    first = take(n)
+    own_st, rec_st = take(2)
+    send_xy, recv_xy, acc = take(n), take(n), take(n)
+    send_z, recv_z, ring = take(n), take(n), take(n)
+    loss_all, stat_all = take(2)
+    core_sems, load_sems, xy_sems, z_sems, right_sems, left_sems, loss_sems, stat_sems = take(8)
+
+    g = lax.axis_index("group")
+    s = lax.axis_index("shard")
+    core = lax.rem(s, 2)
+    chip = s // 2
+    sibling = s + 1 - 2 * core
+
+    barrier = pltpu.get_barrier_semaphore()
+    for e in range(1, shards):
+        pl.semaphore_signal(
+            barrier, 1, device_id=(g, lax.rem(s + e, shards)), device_id_type=MESH
+        )
+    for e in range(1, groups):
+        pl.semaphore_signal(
+            barrier, 1, device_id=(lax.rem(g + e, groups), s), device_id_type=MESH
+        )
+    pl.semaphore_wait(barrier, shards - 1 + groups - 1)
+
+    def remote(src, dst, sems, where, device):
+        return pltpu.make_async_remote_copy(
+            src_ref=src,
+            dst_ref=dst,
+            send_sem=sems.at[(0,) + where],
+            recv_sem=sems.at[(1,) + where],
+            device_id=device,
+            device_id_type=MESH,
+        )
+
+    def core_copy(t, i):
+        c = chunks[t]
+        return remote(
+            pieces[t][i].at[:, 1 - core],
+            first[t].at[:, pl.ds(c.starts[i], c.piece_rows[i])],
+            core_sems,
+            (t, i),
+            (g, sibling),
+        )
+
+    def loss_copy(e):
+        return remote(
+            loss_ref, loss_all.at[g], loss_sems, (e,), (lax.rem(g + e, groups), s)
+        )
+
+    for t in range(n):
+        for i in range(len(chunks[t].names)):
+            core_copy(t, i).start()
+    for e in range(1, groups):
+        loss_copy(e).start()
+    loss_all[g] = loss_ref[...]
+
+    def chip_at(d):
+        return lax.rem(chip + d, chips)
+
+    def loads(t, d):
+        c = chunks[t]
+        q = chip_at(d)
+        return [
+            pltpu.make_async_copy(
+                pieces[t][i].at[q, core],
+                own_st.at[d, pl.ds(c.starts[i], c.piece_rows[i])],
+                load_sems.at[0, d, i],
+            )
+            for i in range(len(c.names))
+        ]
+
+    def late_load(t, d):
+        c = chunks[t]
+        return pltpu.make_async_copy(
+            first[t].at[chip_at(d), pl.ds(0, c.used)],
+            rec_st.at[d, pl.ds(0, c.used)],
+            load_sems.at[1, d, 0],
+        )
+
+    def xy_copy(t, d):
+        return remote(
+            send_xy[t].at[d - 1],
+            recv_xy[t].at[d - 1],
+            xy_sems,
+            (t, d),
+            (g, 2 * chip_at(d) + core),
+        )
+
+    def stage_chips(t):
+        c = chunks[t]
+        order = list(range(1, chips)) + [0]
+        for d in order:
+            for copy in loads(t, d):
+                copy.start()
+        for i in range(len(c.names)):
+            core_copy(t, i).wait_recv()
+        for d in order:
+            late_load(t, d).start()
+        for d in order:
+            for copy in loads(t, d):
+                copy.wait()
+            late_load(t, d).wait()
+            if c.rows > c.used:
+                pad = (c.rows - c.used, D)
+                own_st[d, c.used : c.rows] = jnp.zeros(pad, F32)
+                rec_st[d, c.used : c.rows] = jnp.zeros(pad, F32)
+            if d == 0:
+
+                def keep(rows):
+                    acc[t][rows] = own_st[0, rows] + rec_st[0, rows]
+
+                tiles(c.rows, 32, keep)
+            else:
+
+                def send(rows):
+                    send_xy[t][d - 1, rows] = (own_st[d, rows] + rec_st[d, rows]).astype(c.kind_xy)
+
+                tiles(c.rows, 32, send)
+                xy_copy(t, d).start()
+
+    def part_rows(t, p):
+        return pl.ds(pl.multiple_of(p * chunks[t].part, 16), chunks[t].part)
+
+    def z_copy(t, e):
+        return remote(
+            send_z[t].at[e - 1],
+            recv_z[t].at[e - 1],
+            z_sems,
+            (t, e),
+            (lax.rem(g + e, groups), s),
+        )
+
+    def stage_group(t):
+        c = chunks[t]
+        for d in range(1, chips):
+            xy_copy(t, d).wait_recv()
+
+        def add(rows):
+            total = acc[t][rows]
+            for d in range(1, chips):
+                total = total + recv_xy[t][d - 1, rows].astype(F32)
+            acc[t][rows] = total
+
+        tiles(c.rows, 32, add)
+        for e in range(1, groups):
+            base = pl.multiple_of(lax.rem(g + e, groups) * c.part, 16)
+
+            def send(rows):
+                here = pl.ds(pl.multiple_of(base + rows.start, 16), 16)
+                send_z[t][e - 1, rows] = acc[t][here].astype(BF16)
+
+            tiles(c.part, 16, send)
+            z_copy(t, e).start()
+
+    def ring_copy(t, k, way):
+        p = g - k if way == 0 else g + k
+        side = g + 1 if way == 0 else g - 1
+        sems = right_sems if way == 0 else left_sems
+        rows = part_rows(t, p)
+        return pltpu.make_async_remote_copy(
+            src_ref=ring[t].at[rows],
+            dst_ref=ring[t].at[rows],
+            send_sem=sems.at[0, t, k],
+            recv_sem=sems.at[1, t, k],
+            device_id=(side, s),
+            device_id_type=MESH,
+        )
+
+    def holds(k, way):
+        return g >= k if way == 0 else g + k < groups
+
+    def sends(k, way):
+        return (g >= k) & (g < groups - 1) if way == 0 else (g + k < groups) & (g > 0)
+
+    def arrived(t, k, way):
+        p = g - k if way == 0 else g + k
+        sems = right_sems if way == 0 else left_sems
+        rows = part_rows(t, p)
+        return pltpu.make_async_remote_copy(
+            src_ref=ring[t].at[rows],
+            dst_ref=ring[t].at[rows],
+            send_sem=sems.at[0, t, k],
+            recv_sem=sems.at[1, t, k - 1],
+            device_id=(lax.rem(g + 1, groups), s),
+            device_id_type=MESH,
+        )
+
+    def stage_total(t):
+        c = chunks[t]
+        for e in range(1, groups):
+            z_copy(t, e).wait_recv()
+        base = pl.multiple_of(g * c.part, 16)
+
+        def add(rows):
+            here = pl.ds(pl.multiple_of(base + rows.start, 16), 16)
+            total = acc[t][here]
+            for e in range(1, groups):
+                total = total + recv_z[t][e - 1, rows].astype(F32)
+            ring[t][here] = total.astype(c.kind_z)
+
+        tiles(c.part, 16, add)
+        for way in (0, 1):
+
+            @pl.when(sends(0, way))
+            def _():
+                ring_copy(t, 0, way).start()
+
+    def stage_ring(t, k):
+        for way in (0, 1):
+
+            @pl.when(holds(k, way))
+            def _():
+                arrived(t, k, way).wait_recv()
+
+            if k < groups - 1:
+
+                @pl.when(sends(k, way))
+                def _():
+                    ring_copy(t, k, way).start()
+
+    def stage_end(t, squares):
+        c = chunks[t]
+
+        def once(i, total):
+            rows = pl.ds(pl.multiple_of(i * 16, 16), 16)
+            value = ring[t][rows].astype(F32)
+            outs[t][rows] = value
+            value = value * value
+            return total + value[:8] + value[8:]
+
+        return lax.fori_loop(0, c.rows // 16, once, squares)
+
+    squares = jnp.zeros((8, D), F32)
+    lag = 3 + groups
+    for step in range(n + lag):
+        for behind, stage in enumerate(
+            [stage_chips, stage_group, stage_total]
+            + [functools.partial(stage_ring, k=k) for k in range(1, groups)]
+        ):
+            if 0 <= step - behind < n:
+                stage(step - behind)
+        if 0 <= step - (2 + groups) < n:
+            squares = stage_end(step - (2 + groups), squares)
+
+    for e in range(1, groups):
+        loss_copy(e).wait_recv()
+    loss = loss_all[0]
+    for p in range(1, groups):
+        loss = loss + loss_all[p]
+    lane = lax.broadcasted_iota(jnp.int32, (8, 128), 1)
+    stat_ref[...] = jnp.where(lane == 0, jnp.sum(squares), loss)
+
+    def stat_copy(e):
+        return remote(
+            stat_ref, stat_all.at[s], stat_sems, (e,), (g, lax.rem(s + e, shards))
+        )
+
+    for e in range(1, shards):
+        stat_copy(e).start()
+    stat_all[s] = stat_ref[...]
+    for e in range(1, shards):
+        stat_copy(e).wait_recv()
+    for t in range(n):
+        for i in range(len(chunks[t].names)):
+            core_copy(t, i).wait_send()
+        for d in range(1, chips):
+            xy_copy(t, d).wait_send()
+        for e in range(1, groups):
+            z_copy(t, e).wait_send()
+        for k in range(groups - 1):
+            for way in (0, 1):
+
+                @pl.when(sends(k, way))
+                def _():
+                    ring_copy(t, k, way).wait_send()
+
+    for e in range(1, groups):
+        loss_copy(e).wait_send()
+    for e in range(1, shards):
+        stat_copy(e).wait_send()
+    total = stat_all[0]
+    for p in range(1, shards):
+        total = total + stat_all[p]
+    stat_ref[...] = total
+
+
+def reduce_all(chunks, groups, shards, pieces, loss):
+    chips = shards // 2
+    most = max(c.rows for c in chunks)
+    many = max(len(c.names) for c in chunks)
+    n = len(chunks)
+    hbm = pl.BlockSpec(memory_space=pl.ANY)
+    vmem = pl.BlockSpec(memory_space=pltpu.VMEM)
+    dma = pltpu.SemaphoreType.DMA
+    results = pl.pallas_call(
+        functools.partial(reduce_kernel, chunks, groups, shards),
+        in_specs=[hbm] * sum(len(p) for p in pieces) + [vmem],
+        out_specs=[vmem] * n + [vmem] + [hbm] * n,
+        out_shape=[jax.ShapeDtypeStruct((c.rows, D), F32) for c in chunks]
+        + [jax.ShapeDtypeStruct((8, 128), F32)]
+        + [jax.ShapeDtypeStruct((chips, c.rows, D), F32) for c in chunks],
+        scratch_shapes=[pltpu.VMEM((chips, most, D), F32)] * 2
+        + [pltpu.VMEM((chips - 1, c.rows, D), c.kind_xy) for c in chunks] * 2
+        + [pltpu.VMEM((c.rows, D), F32) for c in chunks]
+        + [pltpu.VMEM((groups - 1, c.part, D), BF16) for c in chunks] * 2
+        + [pltpu.VMEM((c.rows, D), c.kind_z) for c in chunks]
+        + [pltpu.VMEM((groups, 8, 128), F32), pltpu.VMEM((shards, 8, 128), F32)]
+        + [
+            dma((2, n, many)),
+            dma((2, chips, many)),
+            dma((2, n, chips)),
+            dma((2, n, groups)),
+            dma((2, n, groups)),
+            dma((2, n, groups)),
+            dma((2, groups)),
+            dma((2, shards)),
+        ],
+        compiler_params=pltpu.CompilerParams(
+            collective_id=1, has_side_effects=True, vmem_limit_bytes=VMEM_BYTES
+        ),
+        name="reduce",
+    )(*[p for group in pieces for p in group], loss)
+    return results[:n], results[n]
+
+
+def adam_step(weight, grad, moment, square, shrink, scal_ref):
+    grad = grad * scal_ref[0]
+    moment = beta_one * moment + (1.0 - beta_one) * grad
+    square = beta_two * square + (1.0 - beta_two) * grad * grad
+    stepped = moment / scal_ref[1] / (jnp.sqrt(square / scal_ref[2]) + adam_eps)
+    return weight - rate * (stepped + shrink * weight), moment, square
+
+
+def adam_kernel(scal_ref, *refs):
+    w, m, v = refs[0:5], refs[5:10], refs[10:15]
+    g_in, g_qkvo, g_up, g_down, g_head, g_vec = refs[15:21]
+    outs = [refs[21 + 5 * i : 26 + 5 * i] for i in range(4)]
+
+    def update(i, grad, where=...):
+        shrink = 0.0 if i == 4 else decay
+        new = adam_step(w[i][where], grad, m[i][where], v[i][where], shrink, scal_ref)
+        for out, value in zip(outs, new):
+            out[i][where] = value
+        outs[3][i][where] = new[0].astype(BF16)
+
+    update(1, g_qkvo[...], 0)
+    update(1, g_up[...], 1)
+    update(2, g_down[...])
+
+    @pl.when(pl.program_id(0) == 0)
+    def _():
+        update(0, g_in[...])
+        update(3, g_head[...])
+        update(4, g_vec[...])
+
+
+def adam(scalars, weights, moments, seconds, grads):
+    parts = FF // D
+    depth = weights[1].shape[1]
+    tall = weights[2].shape[0] // parts
+
+    def fixed(a):
+        return pl.BlockSpec(a.shape, lambda i: (0,) * a.ndim)
+
+    w_specs = [
+        fixed(weights[0]),
+        pl.BlockSpec((2, depth, D), lambda i: (0, 0, i)),
+        pl.BlockSpec((tall, D), lambda i: (i, 0)),
+        fixed(weights[3]),
+        fixed(weights[4]),
+    ]
+    band = pl.BlockSpec((depth, D), lambda i: (i, 0))
+    g_specs = [fixed(grads[0]), band, band, w_specs[2], fixed(grads[4]), fixed(grads[5])]
+    shapes = [jax.ShapeDtypeStruct(w.shape, F32) for w in weights]
+    low = [jax.ShapeDtypeStruct(w.shape, BF16) for w in weights]
+    outs = pl.pallas_call(
+        adam_kernel,
+        grid=(parts,),
+        in_specs=[pl.BlockSpec(memory_space=pltpu.SMEM)] + w_specs * 3 + g_specs,
+        out_specs=w_specs * 4,
+        out_shape=shapes * 3 + low,
+        compiler_params=params(),
+        name="adam",
+    )(scalars, *weights, *moments, *seconds, *grads)
+    return [outs[i * 5 : (i + 1) * 5] for i in range(4)]
 
 
 def span_mask(length, begins):
@@ -473,67 +897,74 @@
     w0 = lax.all_gather(low[1][0], "shard", axis=0, tiled=True)
     wu = lax.all_gather(low[1][1], "shard", axis=0, tiled=True)
     wd = lax.all_gather(low[2], "shard", axis=0, tiled=True)
-    whead = lax.all_gather(low[3], "shard", axis=1, tiled=True)
-    wh = whead[:D]
-    codes = jnp.pad(whead[D:].astype(F32), ((0, CPAD - CODES), (0, 0)))
-    cu = unit_rows(codes).astype(BF16)
+    whead = lax.all_gather(low[3].T, "shard", axis=0, tiled=True)
+    wh = whead[:, :D]
+    codes = jnp.pad(whead[:, D:].astype(F32), ((0, 0), (0, CPAD - CODES)))
+    codes_root = lax.rsqrt(jnp.sum(codes * codes, 0, keepdims=True) + 1e-06)
+    codes_unit = codes * codes_root
+    cu = codes_unit.astype(BF16)
 
     a, hidden, hid_low, triple = project(x, masked, win, w0, vecs, 256)
     att = attend(lengths, triple)
     loss, z1, act, de, df, z2, dc, dlog, uc, dr1, dy, d_att, gv = feed(
         scale, att, hidden, masked, label, w0, wu, wd, wh, cu, vecs, 256
     )
-    g_lower = product_tn(act, df)
-    g_up = product_tn(z1, de)
-    g_final = product_tn(z2, dc)
-    d_codes_unit = product_tn(dlog, uc)
-    _, codes_back = jax.vjp(unit_rows, codes)
-    g_codes = codes_back(d_codes_unit)[0][:CODES]
+    groups, shards = lax.axis_size("group"), lax.axis_size("shard")
+
+    def split(grad):
+        return grad.reshape(shards // 2, 2, grad.shape[0] // shards, D)
+
+    g_lower = split(product_tn(act, df))
+    g_up = [split(product_tn(z1, de[:, c * D : (c + 1) * D])) for c in range(FF // D)]
+    d_unit = product_tn(uc, dlog)
+    g_codes = codes_root * (d_unit - codes_unit * jnp.sum(d_unit * codes_unit, 0, keepdims=True))
+    g_head = [split(product_tn(dc, z2)), split(jnp.pad(g_codes, ((0, 0), (0, D - CPAD))))]
     dq, dk, dv = attend_back(lengths, triple, d_att)
     dhh, gv = project_back(dq, dk, dv, dr1, masked, x, win, w0, gv, 256)
-    g_block = jnp.concatenate(
-        [
-            product_tn(hid_low, dq),
-            product_tn(hid_low, dk),
-            product_tn(hid_low, dv),
-            product_tn(att, dy),
-        ],
-        1,
+    g_qkvo = [split(product_tn(hid_low, d)) for d in (dq, dk, dv)] + [split(product_tn(att, dy))]
+    wide = FF // shards
+    gv = jnp.swapaxes(gv.reshape(16, shards, wide), 0, 1)
+    gv = jnp.pad(gv, ((0, 0), (0, 0), (0, D - wide))).reshape(shards // 2, 2, 16, D)
+    g_tail = [split(product_tn(a, dhh)), gv]
+    chunks = [
+        Chunk("ht", [CD // shards] * 2, groups, True, True),
+        Chunk("d", [FF // shards], groups, False, True),
+        Chunk("0123", [D // shards] * 4, groups, False, False),
+        Chunk("qkvo", [D // shards] * 4, groups, False, False),
+        Chunk("iv", [CH // shards, 16], groups, False, True),
+    ]
+    (s_head, s_down, s_up, s_qkvo, s_tail), stat = reduce_all(
+        chunks,
+        groups,
+        shards,
+        [g_head, [g_lower], g_up, g_qkvo, g_tail],
+        jnp.broadcast_to(loss, (8, 128)),
     )
-    g_input = product_tn(a, dhh)
-    scattered = (
-        lax.psum_scatter(g_input, "shard", scatter_dimension=0, tiled=True),
-        jnp.stack(
-            [
-                lax.psum_scatter(g_block, "shard", scatter_dimension=0, tiled=True),
-                lax.psum_scatter(g_up, "shard", scatter_dimension=0, tiled=True),
-            ]
-        ),
-        lax.psum_scatter(g_lower, "shard", scatter_dimension=0, tiled=True),
-        lax.psum_scatter(
-            jnp.concatenate([g_final, g_codes], 0), "shard", scatter_dimension=1, tiled=True
-        ),
-        lax.psum_scatter(gv[:NVEC], "shard", scatter_dimension=1, tiled=True),
-    )
-    summed = lax.psum(scattered, "group")
-    loss = lax.psum(loss[0, 0], ("group", "shard")) / count
-    local_squares = sum((jnp.sum(g * g) for g in summed))
-    norm = jnp.sqrt(lax.psum(local_squares, "shard"))
+    norm = jnp.sqrt(stat[0, 0])
+    loss = stat[0, 1] / count
     factor = jnp.minimum(1.0, clip_norm / (norm + 1e-06))
     steps = step_count[0].astype(F32)
     fix_one = 1.0 - jnp.power(beta_one, steps)
     fix_two = 1.0 - jnp.power(beta_two, steps)
-    decays = (decay, decay, decay, decay, 0.0)
-    new_w, new_m, new_v = ([], [], [])
-    for weight, grad, moment, square, shrink in zip(masters, summed, moments, seconds, decays):
-        grad = grad * factor
-        moment = beta_one * moment + (1.0 - beta_one) * grad
-        square = beta_two * square + (1.0 - beta_two) * grad * grad
-        stepped = moment / fix_one / (jnp.sqrt(square / fix_two) + adam_eps)
-        new_w.append(weight - rate * (stepped + shrink * weight))
-        new_m.append(moment)
-        new_v.append(square)
-    copies = [w.astype(BF16) for w in new_w]
+    scalars = jnp.stack([factor, fix_one, fix_two])
+    deep = CD // shards
+    first = CH // shards
+    summed = [
+        s_tail[:first],
+        s_qkvo,
+        s_up,
+        s_down,
+        jnp.concatenate([s_head[:deep], s_head[deep : 2 * deep, :CODES]], 1),
+        s_tail[first : first + NVEC, :wide],
+    ]
+
+    def turned(arrays):
+        return [a.T if i == 3 else a for i, a in enumerate(arrays)]
+
+    new_w, new_m, new_v, copies = (
+        turned(out)
+        for out in adam(scalars, turned(masters), turned(moments), turned(seconds), summed)
+    )
     return (
         *new_w,
         *new_m,

time: 802 us -> 468 us (0.58)
  waiting for transfers between devices: 410 us -> 10.7 us
  Pallas kernels: 124 us -> 291 us
  blocking collectives: 152 us -> 78.7 us
  other arithmetic: 31.3 us -> 6.03 us
    reduce_scatter x5 -> x0, waiting for transfers between devices: 234 us -> none  [the longest x1 80 us: per_device(): lax.psum_scatter(g_lower, 'shard', scatter_dimension=0, tiled=True)]
    pallas_call x0 -> x2, Pallas kernels: none -> 167 us  [the longest x1 155 us: reduce_all(): pl.pallas_call(functools.partial(reduce_kernel, chunks, groups, shards),...]
    psum x1 -> x0, waiting for transfers between devices: 126 us -> none  [per_device(): summed = lax.psum(scattered, 'group')]
    psum x3 -> x0, blocking collectives: 73.6 us -> none  [the longest x1 39.6 us: per_device(): loss = lax.psum(loss[0, 0], ('group', 'shard')) / count]
    unnamed x11 -> x3, waiting for transfers between devices: 39.3 us -> 0.73 us
    dot_general x8 -> x12, matrix products: 23 us -> 40.1 us  [product_tn(): lax.dot_general(left, right, (((0,), (0,)), ((), ())), preferred_element_...]
    unnamed x70 -> x50, local copies, waits for them, and re-layouts: 19.9 us -> 3.03 us
    convert_element_type x6 -> x1, other arithmetic: 14.1 us -> 0.76 us  [per_device(): cu = codes_unit.astype(BF16)]
  transfers between devices with their start and end apart: 10 -> 3, of which waited for: 7 -> 1; matrix products, arithmetic and copies ran while one was open for 5% -> 1% of each run, Pallas kernels for 5% -> 7%
where the time goes in v2:
time: 468 us; the launch traced here: 462 us
  Pallas kernels  291 us (62%)
  blocking collectives  78.7 us (17%)
  matrix products  40.1 us (9%)
  between operations  20.1 us (4%)
  local copies, waits for them, and re-layouts  14.8 us (3%)
  waiting for transfers between devices  10.7 us (2%)
  other arithmetic  6.03 us (1%)
    pallas_call x1, Pallas kernels, reduce_all(): pl.pallas_call(functools.partial(reduce_kernel, chunks, groups, shards),...  155 us
    pallas_call x1, Pallas kernels, feed(): pl.pallas_call(feed_kernel, grid=(n // tile,), in_specs=[pl.BlockSpec(mem...  49.6 us
    psum x1, blocking collectives, per_device(): count = lax.psum(jnp.sum(masked.astype(F32)), ('group', 'shard'))  42.4 us
    dot_general x12, matrix products, product_tn(): lax.dot_general(left, right, (((0,), (0,)), ((), ())), preferred_element_...  40.1 us
    pallas_call x1, Pallas kernels, attend_back(): pl.pallas_call(attend_back_kernel, grid_spec=pltpu.PrefetchScalarGridSpec...  31.1 us
    pallas_call x1, Pallas kernels, attend(): pl.pallas_call(attend_kernel, grid_spec=pltpu.PrefetchScalarGridSpec(num_...  21.3 us
    all_gather x1, blocking collectives, per_device(): win = lax.all_gather(low[0], 'shard', axis=0, tiled=True)  14.7 us
    pallas_call x1, Pallas kernels, adam(): pl.pallas_call(adam_kernel, grid=(parts,), in_specs=[pl.BlockSpec(memory_...  11.9 us
  transfers between devices with their start and end apart: 3, of which 1 were waited for; matrix products, arithmetic and copies ran while one was open for 1% of the time, Pallas kernels for 7%

profile of v2, /device:TPU:0, one launch (start us, length us, event | category | flops | bytes accessed | tf_op | source)
XLA Modules:
  0.0 461.8 jit_solution(729959581302062173)
XLA Ops:
  7.2 1.8 convert_element_type.49
  13.0 42.4 %psum.7 = f32[]{:T(128)} all-reduce(f32[]{:T(128)} %fusion.18), channel_id=1, replica_groups=mesh['group'=4,'shard'=8] {'group','shard'}, use_global_device_ids=true, to_apply=%region_2.3 | all-reduce | flops 1 | bytes 8 | tf_op jit(solution)/shard_map/psum | solution.py:889
  55.4 11.7 %all_gather.23 = bf16[256,1268]{1,0:T(8,128)(2,1)S(1)} all-gather(bf16[32,1268]{1,0:T(8,128)(2,1)S(1)} %convert_bitcast_fusion), channel_id=1, replica_groups=mesh['group'=4,'shard'=8] {'shard'}, dimensions={0}, use_global_device_ids=true | all-gather | bytes 730368 | tf_op jit(solution)/shard_map/all_gather | solution.py:900
  71.6 9.9 %all_gather.20.vec_ref = bf16[14,3072]{1,0:T(8,128)(2,1)} all-gather(bf16[14,384]{1,0:T(8,128)(2,1)S(1)} %convert_element_type.50), channel_id=1, replica_groups=mesh['group'=4,'shard'=8] {'shard'}, dimensions={1}, use_global_device_ids=true | all-gather | bytes 96768 | tf_op jit(solution)/shard_map/all_gather | solution.py:896
  81.5 14.7 %all_gather.18.win_ref = bf16[512,768]{1,0:T(8,128)(2,1)} all-gather(bf16[64,768]{1,0:T(8,128)(2,1)S(1)} %convert_element_type.48), channel_id=1, replica_groups=mesh['group'=4,'shard'=8] {'shard'}, dimensions={0}, use_global_device_ids=true | all-gather | bytes 884736 | tf_op jit(solution)/shard_map/all_gather | solution.py:895
  97.0 10.4 %project.1 = (bf16[1024,512]{1,0:T(8,128)(2,1)}, f32[1024,768]{1,0:T(8,128)}, bf16[1024,768]{1,0:T(8,128)(2,1)}, bf16[1024,2304]{1,0:T(8,128)(2,1)}) custom-call(bf16[1024,512]{1,0:T(8,128)(2,1)} %bitcast.75, f32[1024,1]{1,0:T(8,128)} %bitcast.71, bf16[512,768]{1,0:T(8,128)(2,1)} %all_gather.18.win_ref, bf16[768,3072]{1,0:T(8,128)(2,1)} %bitcast.67, ...), custom_call_target="tpu_custom_call" | custom-call | tf_op jit(solution)/shard_map/project/pallas_call | solution.py:112
  107.4 21.3 %attend.1.att_ref = bf16[1024,768]{1,0:T(8,128)(2,1)} custom-call(s32[2]{0:T(128)} %len_ref.3, bf16[1024,2304]{1,0:T(8,128)(2,1)} %get-tuple-element.70.q_ref.k_ref.v_ref, bf16[1024,2304]{1,0:T(8,128)(2,1)} %get-tuple-element.70.q_ref.k_ref.v_ref, bf16[1024,2304]{1,0:T(8,128)(2,1)} %get-tuple-element.70.q_ref.k_ref.v_ref), custom_call_target="tpu_custom_call" | custom-call | tf_op jit(solution)/shard_map/attend/pallas_call | solution.py:156
  128.7 9.9 %all-gather.6.cloned.1.call-done.wd_ref = bf16[3072,768]{1,0:T(8,128)(2,1)} async-done(((bf16[384,768]{1,0:T(8,128)(2,1)}), bf16[3072,768]{1,0:T(8,128)(2,1)}) %all-gather.6.cloned.1.call-update) | async-done | bytes 4718608 | tf_op jit(solution)/shard_map/all_gather | solution.py:899
  138.6 49.6 %feed.1 = (f32[1,1]{1,0:T(1,128)}, bf16[1024,768]{1,0:T(8,128)(2,1)}, bf16[1024,3072]{1,0:T(8,128)(2,1)}, bf16[1024,3072]{1,0:T(8,128)(2,1)}, bf16[1024,768]{1,0...) custom-call(f32[1]{0:T(128)} %bitcast.scale_ref, ...), custom_call_target="tpu_custom_call" | custom-call | tf_op jit(solution)/shard_map/feed/pallas_call | solution.py:297
  188.2 5.0 %fusion = f32[768,768]{1,0:T(8,128)} fusion(bf16[1024,768]{1,0:T(8,128)(2,1)} %get-tuple-element.78, bf16[1024,3072]{1,0:T(8,128)(2,1)} %get-tuple-element.79), kind=kOutput, calls=%fused_computation | convolution fusion | flops 1207959552 | bytes 5505024 | tf_op jit(solution)/shard_map/dot_general | solution.py:44
  193.2 4.4 fusion.2
  197.6 2.9 fusion.4
  200.4 2.9 fusion.6
  203.3 31.1 %attend_back.1 = (bf16[1024,768]{1,0:T(8,128)(2,1)}, bf16[1024,768]{1,0:T(8,128)(2,1)}, bf16[1024,768]{1,0:T(8,128)(2,1)}) custom-call(s32[2]{0:T(128)} %len_ref.3, bf16[1024,2304]{1,0:T(8,128)(2,1)} %get-tuple-element.70.q_ref.k_ref.v_ref, bf16[1024,2304]{1,0:T(8,128)(2,1)} %get-tuple-element.70.q_ref.k_ref.v_ref, ...), custom_call_target="tpu_custom_call" | custom-call | tf_op jit(solution)/shard_map/attend_back/pallas_call | solution.py:354
  234.5 4.4 fusion.25
  238.9 2.9 fusion.24
  241.8 2.8 fusion.23
  244.6 11.5 %project_back.1 = (bf16[1024,768]{1,0:T(8,128)(2,1)}, f32[16,3072]{1,0:T(8,128)}) custom-call(bf16[1024,768]{1,0:T(8,128)(2,1)} %get-tuple-element.82.dq_ref, bf16[1024,768]{1,0:T(8,128)(2,1)} %get-tuple-element.83.dk_ref, bf16[1024,768]{1,0:T(8,128)(2,1)} %get-tuple-element.84.dv_ref, f32[1024,768]{1,0:T(8,128)} %get-tuple-element.87.dr1_ref, ...), custom_call_target="tpu_custom_call" | custom-call | tf_op jit(solution)/shard_map/project_back/pallas_call | solution.py:402
  260.3 2.8 fusion.26
  263.1 2.2 fusion.27
  265.4 7.9 %fusion.22 = f32[3072,768]{1,0:T(8,128)} fusion(bf16[1024,3072]{1,0:T(8,128)(2,1)S(1)} %bitcast.99, bf16[1024,768]{1,0:T(8,128)(2,1)S(1)} %copy-done.13), kind=kOutput, calls=%fused_computation.36 | convolution fusion | flops 4831838208 | bytes 17301504 | tf_op jit(solution)/shard_map/dot_general | solution.py:44
  276.0 155.4 %reduce.1 = (f32[64,768]{1,0:T(8,128)}, f32[384,768]{1,0:T(8,128)}, f32[384,768]{1,0:T(8,128)}, f32[384,768]{1,0:T(8,128)}, f32[128,768]{1,0:T(8,128)}, /*index=...) custom-call(f32[4,2,32,768]{3,2,1,0:T(8,128)} %bitcast.78, ...), custom_call_target="tpu_custom_call" | custom-call | tf_op jit(solution)/shard_map/reduce/pallas_call | solution.py:761
  433.2 1.6 slice.51.refs_15_
  440.8 11.9 %adam.1 = (f32[64,768]{1,0:T(8,128)}, f32[2,96,3072]{2,1,0:T(8,128)}, f32[384,768]{1,0:T(8,128)}, f32[32,1268]{1,0:T(8,128)}, f32[14,384]{1,0:T(8,128)}, /*index...) custom-call(f32[3]{0:T(128)} %pad_maximum_fusion.1.scal_ref, ...), custom_call_target="tpu_custom_call" | custom-call | tf_op jit(solution)/shard_map/adam/pallas_call | solution.py:842
  (88 shorter events, 20.2 us)
Async XLA Ops:
  7.2 89.8 %all-gather.8.cloned.1.call-start = ((), (), s32[]{:S(2)}) async-start(), calls=%async_computation.1 | async-start | bytes 5308416 | tf_op jit(solution)/shard_map/all_gather | solution.py:897
  9.1 2.0 copy-start.1
  10.2 1.8 copy-start.11
  10.2 45.2 %copy-start.6 = (f32[1268,32]{0,1:T(8,128)S(1)}, f32[1268,32]{0,1:T(8,128)}, u32[]{:S(2)}) copy-start(f32[1268,32]{0,1:T(8,128)} %param.28) | copy-start | bytes 486916
  10.2 118.5 %all-gather.10.cloned.1.call-start = ((), (), s32[]{:S(2)}) async-start(), calls=%async_computation.2 | async-start | bytes 5308416 | tf_op jit(solution)/shard_map/all_gather | solution.py:898
  11.0 127.7 %all-gather.6.cloned.1.call-start = ((), (), s32[]{:S(2)}) async-start(), calls=%async_computation | async-start | bytes 5308416 | tf_op jit(solution)/shard_map/all_gather | solution.py:899
  11.9 57.0 %copy-start.5 = (f32[64,768]{1,0:T(8,128)S(1)}, f32[64,768]{1,0:T(8,128)}, u32[]{:S(2)}) copy-start(f32[64,768]{1,0:T(8,128)} %refs_0_.1) | copy-start | bytes 589828
  12.2 56.8 %copy-start.8 = (f32[14,384]{1,0:T(8,128)S(1)}, f32[14,384]{1,0:T(8,128)}, u32[]{:S(2)}) copy-start(f32[14,384]{1,0:T(8,128)} %refs_4_.1) | copy-start | bytes 64516
  55.4 13.6 %copy-start.10 = (s32[2,512]{1,0:T(2,128)S(1)}, s32[2,512]{1,0:T(2,128)}, u32[]{:S(2)}) copy-start(s32[2,512]{1,0:T(2,128)} %param.23) | copy-start | bytes 12292
  188.2 5.0 %copy-start.12 = (bf16[1024,3072]{1,0:T(8,128)(2,1)S(1)}, bf16[1024,3072]{1,0:T(8,128)(2,1)}, u32[]{:S(2)}) copy-start(bf16[1024,3072]{1,0:T(8,128)(2,1)} %get-tuple-element.79) | copy-start | bytes 18874372
  193.2 4.4 copy-start.17
  203.3 31.1 %copy-start.15 = (bf16[1024,768]{1,0:T(8,128)(2,1)S(1)}, bf16[1024,768]{1,0:T(8,128)(2,1)}, u32[]{:S(2)}) copy-start(bf16[1024,768]{1,0:T(8,128)(2,1)} %get-tuple-element.80) | copy-start | bytes 4718596
  234.5 4.4 copy-start.4
  238.9 2.9 copy-start.3
  244.6 13.2 %copy-start.19 = (bf16[1024,512]{1,0:T(8,128)(2,1)S(1)}, bf16[1024,512]{1,0:T(8,128)(2,1)}, u32[]{:S(2)}) copy-start(bf16[1024,512]{1,0:T(8,128)(2,1)} %get-tuple-element.75) | copy-start | bytes 3145732
  244.6 13.2 %copy-start.20 = (bf16[1024,256]{1,0:T(8,128)(2,1)S(1)}, bf16[1024,256]{1,0:T(8,128)(2,1)}, u32[]{:S(2)}) copy-start(bf16[1024,256]{1,0:T(8,128)(2,1)} %get-tuple-element.74) | copy-start | bytes 1572868
  257.9 5.3 %copy-start.18 = (bf16[1024,512]{1,0:T(8,128)(2,1)S(1)}, bf16[1024,512]{1,0:T(8,128)(2,1)}, u32[]{:S(2)}) copy-start(bf16[1024,512]{1,0:T(8,128)(2,1)} %get-tuple-element.86) | copy-start | bytes 3145732
  258.4 1.9 copy-start
  258.5 6.8 %slice-start = ((s8[6291456]{0:T(1024)(128)(4,1)}), s8[4194304]{0:T(1024)(128)(4,1)S(1)}, s32[]{:S(2)}) async-start(s8[6291456]{0:T(1024)(128)(4,1)} %bitcast.98), calls=%async_computation.3 | async-start | bytes 8388608
  260.3 2.9 copy-start.16
  260.3 5.0 %slice-start.1 = ((s8[6291456]{0:T(1024)(128)(4,1)}), s8[2097152]{0:T(1024)(128)(4,1)S(1)}, s32[]{:S(2)}) async-start(s8[6291456]{0:T(1024)(128)(4,1)} %bitcast.98), calls=%async_computation.4 | async-start | bytes 4194304
  263.1 2.2 copy-start.13
  265.3 7.9 %copy-start.2 = (bf16[1024,768]{1,0:T(8,128)(2,1)S(1)}, bf16[1024,768]{1,0:T(8,128)(2,1)}, u32[]{:S(2)}) copy-start(bf16[1024,768]{1,0:T(8,128)(2,1)} %get-tuple-element.73) | copy-start | bytes 4718596
  265.3 7.9 %copy-start.7 = (bf16[1024,256]{1,0:T(8,128)(2,1)S(1)}, bf16[1024,256]{1,0:T(8,128)(2,1)}, u32[]{:S(2)}) copy-start(bf16[1024,256]{1,0:T(8,128)(2,1)} %get-tuple-element.72) | copy-start | bytes 1572868
  (2 other events, 3.3 us)
Sparse Core Ops, SparseCore 0:
  10.5 42.1 all-gather.7
  55.1 42.1 all-gather.9
  99.8 38.8 all-gather.5

commit v3 on v2

--- a/solution.py
+++ b/solution.py
@@ -322,107 +322,6 @@
     )(scale, att, hidden, masked, label, w0, wu, wd, wh, cu, vecs)
 
 
-def attend_back_kernel(len_ref, q_ref, k_ref, v_ref, do_ref, dq_ref, dk_ref, dv_ref):
-    length = len_ref[pl.program_id(0)]
-    shift = jnp.where(lax.broadcasted_iota(jnp.int32, (LEN, 1), 0) < length, 0.0, -1e30)
-    keys, values = k_ref[...], v_ref[...]
-    dq = dk = dv = None
-    for half in half_masks():
-        query = q_ref[...] * half
-        upstream = do_ref[...] * half
-        scores = product_nt(keys, query) * HEAD_DIM ** (-0.5) + shift
-        power = jnp.exp(scores - jnp.max(scores, 0, keepdims=True))
-        probs = power * (1.0 / jnp.sum(power, 0, keepdims=True))
-        part_v = product(probs.astype(BF16), upstream)
-        d_probs = product_nt(values, upstream)
-        weight = jnp.sum(probs * d_probs, 0, keepdims=True)
-        d_scores = (probs * (d_probs - weight) * HEAD_DIM ** (-0.5)).astype(BF16)
-        part_k = product(d_scores, query)
-        part_q = product_tn(d_scores, keys * half)
-        dq = part_q if dq is None else dq + part_q
-        dk = part_k if dk is None else dk + part_k
-        dv = part_v if dv is None else dv + part_v
-    dq_ref[...] = dq.astype(BF16)
-    dk_ref[...] = dk.astype(BF16)
-    dv_ref[...] = dv.astype(BF16)
-
-
-def attend_back(lengths, triple, d_att):
-    n = triple.shape[0]
-    pairs = D // 128
-    block = pl.BlockSpec((LEN, 128), lambda u, j, _: (u, j))
-    return pl.pallas_call(
-        attend_back_kernel,
-        grid_spec=pltpu.PrefetchScalarGridSpec(
-            num_scalar_prefetch=1,
-            grid=(n // LEN, pairs),
-            in_specs=[
-                block,
-                pl.BlockSpec((LEN, 128), lambda u, j, _: (u, pairs + j)),
-                pl.BlockSpec((LEN, 128), lambda u, j, _: (u, 2 * pairs + j)),
-                block,
-            ],
-            out_specs=[block] * 3,
-        ),
-        out_shape=[jax.ShapeDtypeStruct((n, D), BF16)] * 3,
-        compiler_params=params(),
-        name="attend_back",
-    )(lengths, triple, triple, triple, d_att)
-
-
-def project_back_kernel(
-    dq_ref, dk_ref, dv_ref, dr1_ref, mask_ref, x_ref, win_ref, w0_ref, gvin_ref, dhh_ref, gv_ref
-):
-    @pl.when(pl.program_id(0) == 0)
-    def _():
-        gv_ref[...] = gvin_ref[...]
-
-    dq, dk, dv = dq_ref[...], dk_ref[...], dv_ref[...]
-    gv_ref[4:5, :D] += column_sum(dq.astype(F32))
-    gv_ref[5:6, :D] += column_sum(dv.astype(F32))
-    d_hidden = (
-        dr1_ref[...]
-        + product_nt(dq, w0_ref[:, :D])
-        + product_nt(dk, w0_ref[:, D : 2 * D])
-        + product_nt(dv, w0_ref[:, 2 * D : 3 * D])
-    )
-    masked = mask_ref[...] > 0.0
-    gv_ref[3:4, :D] += column_sum(jnp.where(masked, d_hidden, 0.0))
-    d_proj = jnp.where(masked, 0.0, d_hidden).astype(BF16)
-    dhh_ref[...] = d_proj
-    gv_ref[2:3, :D] += column_sum(d_proj.astype(F32))
-    d_normed = product_nt(d_proj, win_ref[...])
-    hat, _ = norm_parts(x_ref[...].astype(F32))
-    gv_ref[0:1, :CH] += column_sum(d_normed * hat)
-    gv_ref[1:2, :CH] += column_sum(d_normed)
-
-
-def project_back(dq, dk, dv, dr1, masked, x, win, w0, gv, tile):
-    n = x.shape[0]
-    return pl.pallas_call(
-        project_back_kernel,
-        grid=(n // tile,),
-        in_specs=[
-            rows_of(tile, D),
-            rows_of(tile, D),
-            rows_of(tile, D),
-            rows_of(tile, D),
-            rows_of(tile, 1),
-            rows_of(tile, CH),
-            whole((CH, D)),
-            whole((D, FF)),
-            whole((16, FF)),
-        ],
-        out_specs=[rows_of(tile, D), pl.BlockSpec((16, FF), lambda i: (0, 0))],
-        out_shape=[
-            jax.ShapeDtypeStruct((n, D), BF16),
-            jax.ShapeDtypeStruct((16, FF), F32),
-        ],
-        compiler_params=params(),
-        name="project_back",
-    )(dq, dk, dv, dr1, masked, x, win, w0, gv)
-
-
 MESH = pl.DeviceIdType.MESH
 
 
@@ -431,15 +330,33 @@
 
 
 class Chunk:
-    def __init__(self, names, rows, group, wide_xy, wide_z):
-        self.names = names
+    def __init__(self, rows, group, slot, sum_slot, wide_xy, wide_z):
         self.used = sum(rows)
         self.starts = [sum(rows[:i]) for i in range(len(rows))]
-        self.piece_rows = rows
         self.rows = ceil_to(self.used, 16 * group)
         self.part = self.rows // group
+        self.slot = slot
+        self.sum_slot = sum_slot
         self.kind_xy = F32 if wide_xy else BF16
         self.kind_z = F32 if wide_z else BF16
+
+
+HEAD_SLOT = 2
+
+
+def gradient_chunks(groups, shards):
+    down, band = FF // shards, D // shards
+    half = down // 2
+    return [
+        Chunk([half], groups, 0, 0, False, True),
+        Chunk([half], groups, 1, 1, False, True),
+        Chunk([CD // shards] * 2, groups, HEAD_SLOT, 4, True, True),
+        Chunk([band] * 2, groups, 0, 2, False, False),
+        Chunk([band] * 2, groups, 1, 3, False, False),
+        Chunk([band] * 2, groups, 0, 0, False, False),
+        Chunk([band] * 2, groups, 1, 1, False, False),
+        Chunk([CH // shards, 16], groups, 0, 5, False, True),
+    ]
 
 
 def tiles(rows, step, body):
@@ -450,7 +367,7 @@
     lax.fori_loop(0, rows // step, once, 0)
 
 
-def reduce_kernel(chunks, groups, shards, *refs):
+def backward_kernel(chunks, groups, shards, *refs):
     chips = shards // 2
     n = len(chunks)
     refs = list(refs)
@@ -460,22 +377,99 @@
         del refs[:count]
         return out
 
-    pieces = [take(len(c.names)) for c in chunks]
-    (loss_ref,) = take(1)
-    outs = take(n)
+    (
+        act_hbm,
+        df_hbm,
+        z1_hbm,
+        de_hbm,
+        z2_hbm,
+        dc_hbm,
+        uc_hbm,
+        dlog_hbm,
+        triple_hbm,
+        datt_hbm,
+        hid_hbm,
+        att_hbm,
+        dy_hbm,
+        a_hbm,
+        dr1_hbm,
+        x_hbm,
+        w0_hbm,
+        win_hbm,
+        flag_ref,
+        gvin_ref,
+        code_ref,
+        loss_ref,
+    ) = take(22)
+    ring = take(n)
     (stat_ref,) = take(1)
-    first = take(n)
-    own_st, rec_st = take(2)
-    send_xy, recv_xy, acc = take(n), take(n), take(n)
-    send_z, recv_z, ring = take(n), take(n), take(n)
+    pool, heads, dr1_ref, gv_ref = take(4)
+    full = take(3)
+    pair = take(3)
+    send_xy, recv_xy = take(n), take(n)
+    acc = take(6)
+    send_z, recv_z = take(n), take(n)
     loss_all, stat_all = take(2)
-    core_sems, load_sems, xy_sems, z_sems, right_sems, left_sems, loss_sems, stat_sems = take(8)
+    (
+        load_sems,
+        core_sems,
+        credit,
+        xy_sems,
+        z_sems,
+        right_sems,
+        left_sems,
+        loss_sems,
+        stat_sems,
+    ) = take(9)
 
     g = lax.axis_index("group")
     s = lax.axis_index("shard")
     core = lax.rem(s, 2)
     chip = s // 2
     sibling = s + 1 - 2 * core
+    parts = FF // D
+    frames = flag_ref.shape[0]
+
+    def load(src, dst, sem):
+        return pltpu.make_async_copy(src, dst, load_sems.at[sem])
+
+    def cols(ref, c):
+        return ref.at[:, c * D : (c + 1) * D]
+
+    loads = {
+        "df": load(df_hbm, pool.at[0], 0),
+        "z1": load(z1_hbm, pool.at[3], 3),
+        "z2": load(z2_hbm, heads.at[0], 8),
+        "dc": load(dc_hbm, heads.at[1, :, 0:CD], 9),
+        "uc": load(uc_hbm, heads.at[1, :, CD : 2 * CD], 10),
+        "dlog": load(dlog_hbm, heads.at[2, :, 0:CPAD], 11),
+        "hid": load(hid_hbm, pool.at[0], 0),
+        "att": load(att_hbm, pool.at[4], 4),
+        "dy": load(dy_hbm, pool.at[5], 5),
+        "x": load(x_hbm, pool.at[5, :, 0:CH], 5),
+        "win": load(win_hbm, pool.at[6, 0:CH], 6),
+        "dr1": load(dr1_hbm, dr1_ref, 7),
+        "q": load(cols(triple_hbm, 0), heads.at[0], 8),
+        "k": load(cols(triple_hbm, 1), heads.at[1], 9),
+        "v": load(cols(triple_hbm, 2), heads.at[2], 11),
+        "do": load(datt_hbm, heads.at[3], 12),
+        "a": load(a_hbm, heads.at[3, :, 0:CH], 12),
+    }
+    for c in range(parts):
+        loads["act", c] = load(cols(act_hbm, c), pool.at[1 + c % 2], 1 + c % 2)
+        loads["de", c] = load(cols(de_hbm, c), pool.at[1 + c % 2], 1 + c % 2)
+    for c in range(3):
+        loads["w", c] = load(cols(w0_hbm, c), pool.at[1 + c, 0:D], 1 + c)
+
+    def fetch(*names):
+        for name in names:
+            loads[name].start()
+
+    def ready(*names):
+        for name in names:
+            loads[name].wait()
+
+    fetch("df", ("act", 0), ("act", 1), "z2", "dc", "uc", "dlog", "z1", "dr1")
 
     barrier = pltpu.get_barrier_semaphore()
     for e in range(1, shards):
@@ -488,148 +482,140 @@
         )
     pl.semaphore_wait(barrier, shards - 1 + groups - 1)
 
-    def remote(src, dst, sems, where, device):
+    def remote(src, dst, send_sem, recv_sem, device):
         return pltpu.make_async_remote_copy(
             src_ref=src,
             dst_ref=dst,
-            send_sem=sems.at[(0,) + where],
-            recv_sem=sems.at[(1,) + where],
+            send_sem=send_sem,
+            recv_sem=recv_sem,
             device_id=device,
             device_id_type=MESH,
         )
 
-    def core_copy(t, i):
-        c = chunks[t]
-        return remote(
-            pieces[t][i].at[:, 1 - core],
-            first[t].at[:, pl.ds(c.starts[i], c.piece_rows[i])],
-            core_sems,
-            (t, i),
-            (g, sibling),
-        )
-
     def loss_copy(e):
         return remote(
-            loss_ref, loss_all.at[g], loss_sems, (e,), (lax.rem(g + e, groups), s)
+            loss_ref,
+            loss_all.at[g],
+            loss_sems.at[0, e],
+            loss_sems.at[1, e],
+            (lax.rem(g + e, groups), s),
         )
 
-    for t in range(n):
-        for i in range(len(chunks[t].names)):
-            core_copy(t, i).start()
     for e in range(1, groups):
         loss_copy(e).start()
     loss_all[g] = loss_ref[...]
 
+    def core_copy(t):
+        c = chunks[t]
+        return remote(
+            full[c.slot].at[:, 1 - core, 0 : c.used],
+            pair[c.slot].at[:, 0 : c.used],
+            core_sems.at[0, t],
+            core_sems.at[1, t],
+            (g, sibling),
+        )
+
+    before = {}
+    for t, c in enumerate(chunks):
+        earlier = [i for i in range(t) if chunks[i].slot == c.slot]
+        before[t] = earlier[-1] if earlier else None
+    last_of = {c.slot: t for t, c in enumerate(chunks)}
+
+    def free_buffer(t):
+        if before[t] is not None:
+            core_copy(before[t]).wait_send()
+
+    def stage_pair(t):
+        if before[t] is not None:
+            pl.semaphore_wait(credit.at[chunks[t].slot], 1)
+        core_copy(t).start()
+
     def chip_at(d):
         return lax.rem(chip + d, chips)
-
-    def loads(t, d):
-        c = chunks[t]
-        q = chip_at(d)
-        return [
-            pltpu.make_async_copy(
-                pieces[t][i].at[q, core],
-                own_st.at[d, pl.ds(c.starts[i], c.piece_rows[i])],
-                load_sems.at[0, d, i],
-            )
-            for i in range(len(c.names))
-        ]
-
-    def late_load(t, d):
-        c = chunks[t]
-        return pltpu.make_async_copy(
-            first[t].at[chip_at(d), pl.ds(0, c.used)],
-            rec_st.at[d, pl.ds(0, c.used)],
-            load_sems.at[1, d, 0],
-        )
 
     def xy_copy(t, d):
         return remote(
             send_xy[t].at[d - 1],
             recv_xy[t].at[d - 1],
-            xy_sems,
-            (t, d),
+            xy_sems.at[0, t, d],
+            xy_sems.at[1, t, d],
             (g, 2 * chip_at(d) + core),
         )
 
     def stage_chips(t):
         c = chunks[t]
-        order = list(range(1, chips)) + [0]
-        for d in order:
-            for copy in loads(t, d):
-                copy.start()
-        for i in range(len(c.names)):
-            core_copy(t, i).wait_recv()
-        for d in order:
-            late_load(t, d).start()
-        for d in order:
-            for copy in loads(t, d):
-                copy.wait()
-            late_load(t, d).wait()
-            if c.rows > c.used:
-                pad = (c.rows - c.used, D)
-                own_st[d, c.used : c.rows] = jnp.zeros(pad, F32)
-                rec_st[d, c.used : c.rows] = jnp.zeros(pad, F32)
+        own, other = full[c.slot], pair[c.slot]
+        core_copy(t).wait_recv()
+        for d in list(range(1, chips)) + [0]:
+            q = chip_at(d)
             if d == 0:
 
                 def keep(rows):
-                    acc[t][rows] = own_st[0, rows] + rec_st[0, rows]
-
-                tiles(c.rows, 32, keep)
+                    acc[c.sum_slot][rows] = own[q, core, rows] + other[q, rows]
+
+                tiles(c.used, 16, keep)
+                if c.rows > c.used:
+                    acc[c.sum_slot][c.used : c.rows] = jnp.zeros((c.rows - c.used, D), F32)
             else:
 
                 def send(rows):
-                    send_xy[t][d - 1, rows] = (own_st[d, rows] + rec_st[d, rows]).astype(c.kind_xy)
-
-                tiles(c.rows, 32, send)
+                    send_xy[t][d - 1, rows] = (own[q, core, rows] + other[q, rows]).astype(
+                        c.kind_xy
+                    )
+
+                tiles(c.used, 16, send)
                 xy_copy(t, d).start()
-
-    def part_rows(t, p):
-        return pl.ds(pl.multiple_of(p * chunks[t].part, 16), chunks[t].part)
+        if t != last_of[c.slot]:
+            pl.semaphore_signal(
+                credit.at[c.slot], 1, device_id=(g, sibling), device_id_type=MESH
+            )
 
     def z_copy(t, e):
         return remote(
             send_z[t].at[e - 1],
             recv_z[t].at[e - 1],
-            z_sems,
-            (t, e),
+            z_sems.at[0, t, e],
+            z_sems.at[1, t, e],
             (lax.rem(g + e, groups), s),
         )
 
     def stage_group(t):
         c = chunks[t]
+        total_ref = acc[c.sum_slot]
         for d in range(1, chips):
             xy_copy(t, d).wait_recv()
 
         def add(rows):
-            total = acc[t][rows]
+            total = total_ref[rows]
             for d in range(1, chips):
                 total = total + recv_xy[t][d - 1, rows].astype(F32)
-            acc[t][rows] = total
-
-        tiles(c.rows, 32, add)
+            total_ref[rows] = total
+
+        tiles(c.used, 16, add)
         for e in range(1, groups):
             base = pl.multiple_of(lax.rem(g + e, groups) * c.part, 16)
 
             def send(rows):
                 here = pl.ds(pl.multiple_of(base + rows.start, 16), 16)
-                send_z[t][e - 1, rows] = acc[t][here].astype(BF16)
+                send_z[t][e - 1, rows] = total_ref[here].astype(BF16)
 
             tiles(c.part, 16, send)
             z_copy(t, e).start()
 
-    def ring_copy(t, k, way):
+    def part_rows(t, p):
+        return pl.ds(pl.multiple_of(p * chunks[t].part, 16), chunks[t].part)
+
+    def ring_copy(t, k, way, back=0):
         p = g - k if way == 0 else g + k
-        side = g + 1 if way == 0 else g - 1
+        side = lax.rem(g + 1, groups) if way == 0 else lax.rem(g + groups - 1, groups)
         sems = right_sems if way == 0 else left_sems
         rows = part_rows(t, p)
-        return pltpu.make_async_remote_copy(
-            src_ref=ring[t].at[rows],
-            dst_ref=ring[t].at[rows],
-            send_sem=sems.at[0, t, k],
-            recv_sem=sems.at[1, t, k],
-            device_id=(side, s),
-            device_id_type=MESH,
+        return remote(
+            ring[t].at[rows],
+            ring[t].at[rows],
+            sems.at[0, t, k],
+            sems.at[1, t, k - back],
+            (side, s),
         )
 
     def holds(k, way):
@@ -638,28 +624,16 @@
     def sends(k, way):
         return (g >= k) & (g < groups - 1) if way == 0 else (g + k < groups) & (g > 0)
 
-    def arrived(t, k, way):
-        p = g - k if way == 0 else g + k
-        sems = right_sems if way == 0 else left_sems
-        rows = part_rows(t, p)
-        return pltpu.make_async_remote_copy(
-            src_ref=ring[t].at[rows],
-            dst_ref=ring[t].at[rows],
-            send_sem=sems.at[0, t, k],
-            recv_sem=sems.at[1, t, k - 1],
-            device_id=(lax.rem(g + 1, groups), s),
-            device_id_type=MESH,
-        )
-
     def stage_total(t):
         c = chunks[t]
+        total_ref = acc[c.sum_slot]
         for e in range(1, groups):
             z_copy(t, e).wait_recv()
         base = pl.multiple_of(g * c.part, 16)
 
         def add(rows):
             here = pl.ds(pl.multiple_of(base + rows.start, 16), 16)
-            total = acc[t][here]
+            total = total_ref[here]
             for e in range(1, groups):
                 total = total + recv_z[t][e - 1, rows].astype(F32)
             ring[t][here] = total.astype(c.kind_z)
@@ -676,7 +650,7 @@
 
             @pl.when(holds(k, way))
             def _():
-                arrived(t, k, way).wait_recv()
+                ring_copy(t, k, way, 1).wait_recv()
 
             if k < groups - 1:
 
@@ -688,25 +662,189 @@
         c = chunks[t]
 
         def once(i, total):
-            rows = pl.ds(pl.multiple_of(i * 16, 16), 16)
-            value = ring[t][rows].astype(F32)
-            outs[t][rows] = value
+            value = ring[t][pl.ds(pl.multiple_of(i * 16, 16), 16)].astype(F32)
             value = value * value
             return total + value[:8] + value[8:]
 
         return lax.fori_loop(0, c.rows // 16, once, squares)
 
-    squares = jnp.zeros((8, D), F32)
-    lag = 3 + groups
-    for step in range(n + lag):
-        for behind, stage in enumerate(
-            [stage_chips, stage_group, stage_total]
-            + [functools.partial(stage_ring, k=k) for k in range(1, groups)]
-        ):
-            if 0 <= step - behind < n:
-                stage(step - behind)
-        if 0 <= step - (2 + groups) < n:
-            squares = stage_end(step - (2 + groups), squares)
+    done = [0] * n
+    squares = [jnp.zeros((8, D), F32)]
+
+    def step(t):
+        now = done[t]
+        done[t] += 1
+        if now == 0:
+            stage_pair(t)
+        elif now == 1:
+            stage_chips(t)
+        elif now == 2:
+            stage_group(t)
+        elif now == 3:
+            stage_total(t)
+        elif now < 3 + groups:
+            stage_ring(t, now - 3)
+        else:
+            squares[0] = stage_end(t, squares[0])
+
+    def scatter(value, slots, at, per, first_shard):
+        count = value.shape[0] // per
+        each = per // len(slots)
+        for k in range(count):
+            shard = first_shard * 1 + k
+            for i, slot in enumerate(slots):
+                rows = value[k * per + i * each : k * per + (i + 1) * each]
+                full[slot][shard // 2, lax.rem(shard, 2), at : at + each, 0 : rows.shape[1]] = rows
+
+    def grad(left, right, slots, at, per, block):
+        width = left.shape[1]
+
+        def once(i, carry):
+            some = left[:, pl.ds(pl.multiple_of(i * block, 128), block)]
+            scatter(product_tn(some, right[...]), slots, at, per, i * (block // per))
+            return carry
+
+        lax.fori_loop(0, width // block, once, 0)
+
+    down, band, deep, first = FF // shards, D // shards, CD // shards, CH // shards
+    wide = FF // shards
+    pairs = D // 128
+
+    ready("df")
+    for c in range(parts):
+        ready(("act", c))
+        for i in range(2):
+            value = product_tn(
+                pool[1 + c % 2, :, i * (D // 2) : (i + 1) * (D // 2)], pool[0]
+            )
+            scatter(value, [0, 1], 0, down, (c * D + i * (D // 2)) // down)
+        if c + 2 < parts:
+            fetch(("act", c + 2))
+        else:
+            fetch(("de", c - 2))
+    step(0)
+    step(1)
+    fetch("hid")
+    ready("z2", "dc", "uc", "dlog")
+    scatter(product_tn(heads[1, :, 0:CD], heads[0]), [HEAD_SLOT], 0, deep, 0)
+    d_unit = product_tn(heads[1, :, CD : 2 * CD], heads[2, :, 0:CPAD])
+    codes = code_ref[...]
+    root = lax.rsqrt(jnp.sum(codes * codes, 0, keepdims=True) + 1e-06)
+    unit = codes * root
+    d_codes = root * (d_unit - unit * jnp.sum(d_unit * unit, 0, keepdims=True))
+    scatter(d_codes, [HEAD_SLOT], deep, deep, 0)
+    full[HEAD_SLOT][:, :, deep : 2 * deep, CPAD:D] = jnp.zeros((chips, 2, deep, D - CPAD), F32)
+    step(2)
+    fetch("q", "k", "v", "do", "att", "dy", "win")
+    step(0)
+    step(1)
+    ready("z1")
+    for t, first_part in ((3, 0), (4, 2)):
+        free_buffer(t)
+        for i in range(2):
+            c = first_part + i
+            ready(("de", c))
+            grad(pool.at[3], pool.at[1 + c % 2], [chunks[t].slot], i * band, band, D // 2)
+            if c + 2 < parts:
+                fetch(("de", c + 2))
+        step(t)
+    for c in range(3):
+        fetch(("w", c))
+
+    halves = half_masks()
+
+    def attention(i, carry):
+        rows = pl.ds(pl.multiple_of((i // pairs) * LEN, LEN), LEN)
+        lanes = pl.ds(pl.multiple_of(lax.rem(i, pairs) * 128, 128), 128)
+        shift = flag_ref[rows, 1:2]
+        keys, values = heads[1, rows, lanes], heads[2, rows, lanes]
+        dq = dk = dv = None
+        for half in halves:
+            query = heads[0, rows, lanes] * half
+            upstream = heads[3, rows, lanes] * half
+            scores = product_nt(keys, query) * HEAD_DIM ** (-0.5) + shift
+            power = jnp.exp(scores - jnp.max(scores, 0, keepdims=True))
+            probs = power * (1.0 / jnp.sum(power, 0, keepdims=True))
+            part_v = product(probs.astype(BF16), upstream)
+            d_probs = product_nt(values, upstream)
+            weight = jnp.sum(probs * d_probs, 0, keepdims=True)
+            d_scores = (probs * (d_probs - weight) * HEAD_DIM ** (-0.5)).astype(BF16)
+            part_k = product(d_scores, query)
+            part_q = product_tn(d_scores, keys * half)
+            dq = part_q if dq is None else dq + part_q
+            dk = part_k if dk is None else dk + part_k
+            dv = part_v if dv is None else dv + part_v
+        heads[0, rows, lanes] = dq.astype(BF16)
+        heads[1, rows, lanes] = dk.astype(BF16)
+        heads[2, rows, lanes] = dv.astype(BF16)
+        return carry
+
+    ready("q", "k", "v", "do")
+    rounds = (frames // LEN) * pairs
+    plan = [(3, 4, 2), (0,), (1, 0), (0, 1), (0, 1)]
+    cut = [rounds * i // len(plan) for i in range(len(plan) + 1)]
+    for i, some in enumerate(plan):
+        lax.fori_loop(cut[i], cut[i + 1], attention, 0)
+        for t in some:
+            step(t)
+    fetch("a")
+
+    ready("hid", "att", "dy")
+    free_buffer(5)
+    grad(pool.at[0], heads.at[0], [0], 0, band, D // 2)
+    grad(pool.at[0], heads.at[1], [0], band, band, D // 2)
+    step(5)
+    free_buffer(6)
+    grad(pool.at[0], heads.at[2], [1], 0, band, D // 2)
+    grad(pool.at[4], pool.at[5], [1], band, band, D // 2)
+    step(6)
+    fetch("x")
+    step(5)
+    step(3)
+    step(6)
+    ready(("w", 0), ("w", 1), ("w", 2), "win", "dr1", "x")
+
+    gv_ref[...] = gvin_ref[...]
+
+    def back(i, carry):
+        rows = pl.ds(pl.multiple_of(i * 256, 256), 256)
+        dq, dk, dv = heads[0, rows], heads[1, rows], heads[2, rows]
+        gv_ref[4:5, :D] += column_sum(dq.astype(F32))
+        gv_ref[5:6, :D] += column_sum(dv.astype(F32))
+        d_hidden = (
+            dr1_ref[rows]
+            + product_nt(dq, pool[1, 0:D])
+            + product_nt(dk, pool[2, 0:D])
+            + product_nt(dv, pool[3, 0:D])
+        )
+        masked = flag_ref[rows, 0:1] > 0.0
+        gv_ref[3:4, :D] += column_sum(jnp.where(masked, d_hidden, 0.0))
+        d_proj = jnp.where(masked, 0.0, d_hidden).astype(BF16)
+        pool[4, rows] = d_proj
+        gv_ref[2:3, :D] += column_sum(d_proj.astype(F32))
+        d_normed = product_nt(d_proj, pool[6, 0:CH])
+        hat, _ = norm_parts(pool[5, rows, 0:CH].astype(F32))
+        gv_ref[0:1, :CH] += column_sum(d_normed * hat)
+        gv_ref[1:2, :CH] += column_sum(d_normed)
+        return carry
+
+    lax.fori_loop(0, frames // 256, back, 0)
+    ready("a")
+    free_buffer(7)
+    grad(heads.at[3, :, 0:CH], pool.at[4], [0], 0, first, CH // 2)
+    for b in range(shards):
+        full[0][b // 2, b % 2, first : first + 16, 0:wide] = gv_ref[:, b * wide : (b + 1) * wide]
+        full[0][b // 2, b % 2, first : first + 16, wide:D] = jnp.zeros((16, D - wide), F32)
+    step(7)
+    step(4)
+    step(7)
+    order = [0, 1, 3, 4, 2, 5, 6, 7]
+    final = 4 + groups
+    while min(done) < final:
+        for i, t in enumerate(order):
+            ahead = [done[u] for u in order[:i]]
+            if done[t] < final and all(d > done[t] for d in ahead if d < final):
+                step(t)
 
     for e in range(1, groups):
         loss_copy(e).wait_recv()
@@ -714,11 +852,15 @@
     for p in range(1, groups):
         loss = loss + loss_all[p]
     lane = lax.broadcasted_iota(jnp.int32, (8, 128), 1)
-    stat_ref[...] = jnp.where(lane == 0, jnp.sum(squares), loss)
+    stat_ref[...] = jnp.where(lane == 0, jnp.sum(squares[0]), loss)
 
     def stat_copy(e):
         return remote(
-            stat_ref, stat_all.at[s], stat_sems, (e,), (g, lax.rem(s + e, shards))
+            stat_ref,
+            stat_all.at[s],
+            stat_sems.at[0, e],
+            stat_sems.at[1, e],
+            (g, lax.rem(s + e, shards)),
         )
 
     for e in range(1, shards):
@@ -727,8 +869,8 @@
     for e in range(1, shards):
         stat_copy(e).wait_recv()
     for t in range(n):
-        for i in range(len(chunks[t].names)):
-            core_copy(t, i).wait_send()
+        if t == last_of[chunks[t].slot]:
+            core_copy(t).wait_send()
         for d in range(1, chips):
             xy_copy(t, d).wait_send()
         for e in range(1, groups):
@@ -750,30 +892,38 @@
     stat_ref[...] = total
 
 
-def reduce_all(chunks, groups, shards, pieces, loss):
+def backward(groups, shards, operands, small):
+    chunks = gradient_chunks(groups, shards)
     chips = shards // 2
-    most = max(c.rows for c in chunks)
-    many = max(len(c.names) for c in chunks)
     n = len(chunks)
+    frames = operands[0].shape[0]
     hbm = pl.BlockSpec(memory_space=pl.ANY)
     vmem = pl.BlockSpec(memory_space=pltpu.VMEM)
     dma = pltpu.SemaphoreType.DMA
+    deepest = [max(c.used for c in chunks if c.slot == i) for i in range(3)]
+    sums = [max(c.rows for c in chunks if c.sum_slot == i) for i in range(6)]
     results = pl.pallas_call(
-        functools.partial(reduce_kernel, chunks, groups, shards),
-        in_specs=[hbm] * sum(len(p) for p in pieces) + [vmem],
-        out_specs=[vmem] * n + [vmem] + [hbm] * n,
-        out_shape=[jax.ShapeDtypeStruct((c.rows, D), F32) for c in chunks]
-        + [jax.ShapeDtypeStruct((8, 128), F32)]
-        + [jax.ShapeDtypeStruct((chips, c.rows, D), F32) for c in chunks],
-        scratch_shapes=[pltpu.VMEM((chips, most, D), F32)] * 2
-        + [pltpu.VMEM((chips - 1, c.rows, D), c.kind_xy) for c in chunks] * 2
-        + [pltpu.VMEM((c.rows, D), F32) for c in chunks]
+        functools.partial(backward_kernel, chunks, groups, shards),
+        in_specs=[hbm] * len(operands) + [vmem] * len(small),
+        out_specs=[vmem] * (n + 1),
+        out_shape=[jax.ShapeDtypeStruct((c.rows, D), c.kind_z) for c in chunks]
+        + [jax.ShapeDtypeStruct((8, 128), F32)],
+        scratch_shapes=[
+            pltpu.VMEM((7, frames, D), BF16),
+            pltpu.VMEM((4, frames, D), BF16),
+            pltpu.VMEM((frames, D), F32),
+            pltpu.VMEM((16, FF), F32),
+        ]
+        + [pltpu.VMEM((chips, 2, rows, D), F32) for rows in deepest]
+        + [pltpu.VMEM((chips, rows, D), F32) for rows in deepest]
+        + [pltpu.VMEM((chips - 1, c.used, D), c.kind_xy) for c in chunks] * 2
+        + [pltpu.VMEM((rows, D), F32) for rows in sums]
         + [pltpu.VMEM((groups - 1, c.part, D), BF16) for c in chunks] * 2
-        + [pltpu.VMEM((c.rows, D), c.kind_z) for c in chunks]
         + [pltpu.VMEM((groups, 8, 128), F32), pltpu.VMEM((shards, 8, 128), F32)]
         + [
-            dma((2, n, many)),
-            dma((2, chips, many)),
+            dma((13,)),
+            dma((2, n)),
+            pltpu.SemaphoreType.REGULAR((3,)),
             dma((2, n, chips)),
             dma((2, n, groups)),
             dma((2, n, groups)),
@@ -782,10 +932,10 @@
             dma((2, shards)),
         ],
         compiler_params=pltpu.CompilerParams(
-            collective_id=1, has_side_effects=True, vmem_limit_bytes=VMEM_BYTES
+            collective_id=1, has_side_effects=True, vmem_limit_bytes=64 * 1024 * 1024 - 65536
         ),
-        name="reduce",
-    )(*[p for group in pieces for p in group], loss)
+        name="backward",
+    )(*operands, *small)
     return results[:n], results[n]
 
 
@@ -809,8 +959,8 @@
             out[i][where] = value
         outs[3][i][where] = new[0].astype(BF16)
 
-    update(1, g_qkvo[...], 0)
-    update(1, g_up[...], 1)
+    update(1, g_qkvo[...].astype(F32), 0)
+    update(1, g_up[...].astype(F32), 1)
     update(2, g_down[...])
 
     @pl.when(pl.program_id(0) == 0)
@@ -910,35 +1060,13 @@
         scale, att, hidden, masked, label, w0, wu, wd, wh, cu, vecs, 256
     )
     groups, shards = lax.axis_size("group"), lax.axis_size("shard")
-
-    def split(grad):
-        return grad.reshape(shards // 2, 2, grad.shape[0] // shards, D)
-
-    g_lower = split(product_tn(act, df))
-    g_up = [split(product_tn(z1, de[:, c * D : (c + 1) * D])) for c in range(FF // D)]
-    d_unit = product_tn(uc, dlog)
-    g_codes = codes_root * (d_unit - codes_unit * jnp.sum(d_unit * codes_unit, 0, keepdims=True))
-    g_head = [split(product_tn(dc, z2)), split(jnp.pad(g_codes, ((0, 0), (0, D - CPAD))))]
-    dq, dk, dv = attend_back(lengths, triple, d_att)
-    dhh, gv = project_back(dq, dk, dv, dr1, masked, x, win, w0, gv, 256)
-    g_qkvo = [split(product_tn(hid_low, d)) for d in (dq, dk, dv)] + [split(product_tn(att, dy))]
-    wide = FF // shards
-    gv = jnp.swapaxes(gv.reshape(16, shards, wide), 0, 1)
-    gv = jnp.pad(gv, ((0, 0), (0, 0), (0, D - wide))).reshape(shards // 2, 2, 16, D)
-    g_tail = [split(product_tn(a, dhh)), gv]
-    chunks = [
-        Chunk("ht", [CD // shards] * 2, groups, True, True),
-        Chunk("d", [FF // shards], groups, False, True),
-        Chunk("0123", [D // shards] * 4, groups, False, False),
-        Chunk("qkvo", [D // shards] * 4, groups, False, False),
-        Chunk("iv", [CH // shards, 16], groups, False, True),
-    ]
-    (s_head, s_down, s_up, s_qkvo, s_tail), stat = reduce_all(
-        chunks,
+    position = lax.broadcasted_iota(jnp.int32, (utters, LEN), 1)
+    shift = jnp.where(position < lengths[:, None], 0.0, -1e30).reshape(n, 1)
+    sums, stat = backward(
         groups,
         shards,
-        [g_head, [g_lower], g_up, g_qkvo, g_tail],
-        jnp.broadcast_to(loss, (8, 128)),
+        [act, df, z1, de, z2, dc, uc, dlog, triple, d_att, hid_low, att, dy, a, dr1, x, w0, win],
+        [jnp.concatenate([masked, shift], 1), gv, codes, jnp.broadcast_to(loss, (8, 128))],
     )
     norm = jnp.sqrt(stat[0, 0])
     loss = stat[0, 1] / count
@@ -947,15 +1075,19 @@
     fix_one = 1.0 - jnp.power(beta_one, steps)
     fix_two = 1.0 - jnp.power(beta_two, steps)
     scalars = jnp.stack([factor, fix_one, fix_two])
-    deep = CD // shards
-    first = CH // shards
+    deep, band, first, wide = CD // shards, D // shards, CH // shards, FF // shards
+
+    def bands(a, b):
+        return jnp.concatenate([a[: 2 * band], b[: 2 * band]], 0)
+
+    half = wide // 2
     summed = [
-        s_tail[:first],
-        s_qkvo,
-        s_up,
-        s_down,
-        jnp.concatenate([s_head[:deep], s_head[deep : 2 * deep, :CODES]], 1),
-        s_tail[first : first + NVEC, :wide],
+        sums[7][:first],
+        bands(sums[5], sums[6]),
+        bands(sums[3], sums[4]),
+        jnp.concatenate([sums[0][:half], sums[1][:half]], 0),
+        jnp.concatenate([sums[2][:deep], sums[2][deep : 2 * deep, :CODES]], 1),
+        sums[7][first : first + NVEC, :wide],
     ]
 
     def turned(arrays):

time: 468 us -> 375 us (0.80)
  Pallas kernels: 291 us -> 239 us
  matrix products: 40.1 us -> 0 us
    pallas_call x3 -> x1, Pallas kernels: 198 us -> 146 us  [backward(): pl.pallas_call(functools.partial(backward_kernel, chunks, groups, shards)...]
    dot_general x12 -> x0, matrix products: 40.1 us -> none  [product_tn(): lax.dot_general(left, right, (((0,), (0,)), ((), ())), preferred_element_...]
  transfers between devices with their start and end apart: 3 -> 3, of which waited for: 1 -> 1; matrix products, arithmetic and copies ran while one was open for 1% -> 2% of each run, Pallas kernels for 7% -> 9%
where the time goes in v3:
time: 375 us; the launch traced here: 369 us
  Pallas kernels  239 us (64%)
  blocking collectives  77.6 us (21%)
  between operations  20.2 us (5%)
  local copies, waits for them, and re-layouts  12.4 us (3%)
  other arithmetic  10.2 us (3%)
  waiting for transfers between devices  9.96 us (3%)
    pallas_call x1, Pallas kernels, backward(): pl.pallas_call(functools.partial(backward_kernel, chunks, groups, shards)...  146 us
    pallas_call x1, Pallas kernels, feed(): pl.pallas_call(feed_kernel, grid=(n // tile,), in_specs=[pl.BlockSpec(mem...  49.2 us
    psum x1, blocking collectives, per_device(): count = lax.psum(jnp.sum(masked.astype(F32)), ('group', 'shard'))  42.4 us
    pallas_call x1, Pallas kernels, attend(): pl.pallas_call(attend_kernel, grid_spec=pltpu.PrefetchScalarGridSpec(num_...  21.3 us
    all_gather x1, blocking collectives, per_device(): win = lax.all_gather(low[0], 'shard', axis=0, tiled=True)  13.7 us
    pallas_call x1, Pallas kernels, adam(): pl.pallas_call(adam_kernel, grid=(parts,), in_specs=[pl.BlockSpec(memory_...  11.7 us
    all_gather x1, blocking collectives, per_device(): whead = lax.all_gather(low[3].T, 'shard', axis=0, tiled=True)  11.6 us
    pallas_call x1, Pallas kernels, project(): pl.pallas_call(project_kernel, grid=(n // tile,), in_specs=[rows_of(tile,...  10.4 us
  transfers between devices with their start and end apart: 3, of which 1 were waited for; matrix products, arithmetic and copies ran while one was open for 2% of the time, Pallas kernels for 9%

profile of v3, /device:TPU:0, one launch (start us, length us, event | category | flops | bytes accessed | tf_op | source)
XLA Modules:
  0.0 369.1 jit_solution(8728644368829141842)
XLA Ops:
  7.2 1.8 convert_element_type.45
  9.1 1.1 fusion.4
  11.0 0.9 convert_element_type.47
  13.0 42.4 %psum.7 = f32[]{:T(128)} all-reduce(f32[]{:T(128)} %get-tuple-element.121), channel_id=1, replica_groups=mesh['group'=4,'shard'=8] {'group','shard'}, use_global_device_ids=true, to_apply=%region_2.3 | all-reduce | flops 1 | bytes 8 | tf_op jit(solution)/shard_map/psum | solution.py:1039
  55.4 11.6 %all_gather.23 = bf16[256,1268]{1,0:T(8,128)(2,1)S(1)} all-gather(bf16[32,1268]{1,0:T(8,128)(2,1)S(1)} %convert_bitcast_fusion), channel_id=1, replica_groups=mesh['group'=4,'shard'=8] {'shard'}, dimensions={0}, use_global_device_ids=true | all-gather | bytes 730368 | tf_op jit(solution)/shard_map/all_gather | solution.py:1050
  67.9 1.0 copy.51.mask_ref
  69.0 1.0 copy.57
  70.1 1.0 copy.54.refs_18_
  72.6 9.9 %all_gather.20.vec_ref = bf16[14,3072]{1,0:T(8,128)(2,1)} all-gather(bf16[14,384]{1,0:T(8,128)(2,1)S(1)} %convert_element_type.46), channel_id=1, replica_groups=mesh['group'=4,'shard'=8] {'shard'}, dimensions={1}, use_global_device_ids=true | all-gather | bytes 96768 | tf_op jit(solution)/shard_map/all_gather | solution.py:1046
  83.3 13.7 %all_gather.18.win_ref.refs_17_ = bf16[512,768]{1,0:T(8,128)(2,1)} all-gather(bf16[64,768]{1,0:T(8,128)(2,1)S(1)} %convert_element_type.44), channel_id=1, replica_groups=mesh['group'=4,'shard'=8] {'shard'}, dimensions={0}, use_global_device_ids=true | all-gather | bytes 884736 | tf_op jit(solution)/shard_map/all_gather | solution.py:1045
  97.8 10.4 %project.1 = (bf16[1024,512]{1,0:T(8,128)(2,1)}, f32[1024,768]{1,0:T(8,128)}, bf16[1024,768]{1,0:T(8,128)(2,1)}, bf16[1024,2304]{1,0:T(8,128)(2,1)}) custom-call(bf16[1024,512]{1,0:T(8,128)(2,1)} %bitcast.36, f32[1024,1]{1,0:T(8,128)} %copy.51.mask_ref, bf16[512,768]{1,0:T(8,128)(2,1)} %all_gather.18.win_ref.refs_17_, bf16[768,3072]{1,0:T(8,128)(2,1)} %bitcast.32, ...), custom_call_target="tpu_custom_call" | custom-call | tf_op jit(solution)/shard_map/project/pallas_call | solution.py:112
  108.1 21.3 %attend.1.att_ref.refs_11_ = bf16[1024,768]{1,0:T(8,128)(2,1)} custom-call(s32[2]{0:T(128)} %len_ref.1, bf16[1024,2304]{1,0:T(8,128)(2,1)} %get-tuple-element.68.q_ref.k_ref.v_ref.refs_8_, bf16[1024,2304]{1,0:T(8,128)(2,1)} %get-tuple-element.68.q_ref.k_ref.v_ref.refs_8_, bf16[1024,2304]{1,0:T(8,128)(2,1)} %get-tuple-element.68.q_ref.k_ref.v_ref.refs_8_), custom_call_target="tpu_custom_call" | custom-call | tf_op jit(solution)/shard_map/attend/pallas_call | solution.py:156
  129.4 9.2 %all-gather.6.cloned.1.call-done.wd_ref = bf16[3072,768]{1,0:T(8,128)(2,1)} async-done(((bf16[384,768]{1,0:T(8,128)(2,1)}), bf16[3072,768]{1,0:T(8,128)(2,1)}) %all-gather.6.cloned.1.call-update) | async-done | bytes 4718608 | tf_op jit(solution)/shard_map/all_gather | solution.py:1049
  138.6 49.2 %feed.1 = (f32[1,1]{1,0:T(1,128)}, bf16[1024,768]{1,0:T(8,128)(2,1)}, bf16[1024,3072]{1,0:T(8,128)(2,1)}, bf16[1024,3072]{1,0:T(8,128)(2,1)}, bf16[1024,768]{1,0...) custom-call(f32[1]{0:T(128)} %bitcast.scale_ref, ...), custom_call_target="tpu_custom_call" | custom-call | tf_op jit(solution)/shard_map/feed/pallas_call | solution.py:297
  187.9 1.2 broadcast_in_dim.35.refs_21_
  189.1 145.9 %backward.1 = (f32[192,768]{1,0:T(8,128)}, f32[192,768]{1,0:T(8,128)}, f32[64,768]{1,0:T(8,128)}, bf16[192,768]{1,0:T(8,128)(2,1)}, bf16[192,768]{1,0:T(8,128)(2...) custom-call(bf16[1024,3072]{1,0:T(8,128)(2,1)} %get-tuple-element.70.refs_0_, ...), custom_call_target="tpu_custom_call" | custom-call | tf_op jit(solution)/shard_map/backward/pallas_call | solution.py:905
  335.1 0.9 slice.36
  336.0 0.8 slice.37
  336.9 1.7 slice.35.refs_15_
  338.6 1.3 slice.38.refs_20_
  339.9 1.3 fusion.5
  343.9 2.4 pad_maximum_fusion.refs_18_
  347.0 1.1 pad_maximum_fusion.1
  348.1 11.7 %adam.1 = (f32[64,768]{1,0:T(8,128)}, f32[2,96,3072]{2,1,0:T(8,128)}, f32[384,768]{1,0:T(8,128)}, f32[32,1268]{1,0:T(8,128)}, f32[14,384]{1,0:T(8,128)}, /*index...) custom-call(f32[3]{0:T(128)} %pad_maximum_fusion.5.scal_ref, ...), custom_call_target="tpu_custom_call" | custom-call | tf_op jit(solution)/shard_map/adam/pallas_call | solution.py:992
  (51 shorter events, 5.8 us)
Async XLA Ops:
  7.2 90.6 %all-gather.8.cloned.1.call-start = ((), (), s32[]{:S(2)}) async-start(), calls=%async_computation.1 | async-start | bytes 5308416 | tf_op jit(solution)/shard_map/all_gather | solution.py:1047
  9.1 2.0 copy-start
  10.2 1.7 copy-start.8
  10.2 1.8 copy-start.10
  10.2 45.2 %copy-start.2 = (f32[1268,32]{0,1:T(8,128)S(1)}, f32[1268,32]{0,1:T(8,128)}, u32[]{:S(2)}) copy-start(f32[1268,32]{0,1:T(8,128)} %param.28) | copy-start | bytes 486916
  10.2 119.2 %all-gather.10.cloned.1.call-start = ((), (), s32[]{:S(2)}) async-start(), calls=%async_computation.2 | async-start | bytes 5308416 | tf_op jit(solution)/shard_map/all_gather | solution.py:1048
  11.0 127.7 %all-gather.6.cloned.1.call-start = ((), (), s32[]{:S(2)}) async-start(), calls=%async_computation | async-start | bytes 5308416 | tf_op jit(solution)/shard_map/all_gather | solution.py:1049
  11.9 57.0 %copy-start.1 = (f32[64,768]{1,0:T(8,128)S(1)}, f32[64,768]{1,0:T(8,128)}, u32[]{:S(2)}) copy-start(f32[64,768]{1,0:T(8,128)} %refs_0_.1) | copy-start | bytes 589828
  12.3 56.7 %copy-start.7 = (f32[14,384]{1,0:T(8,128)S(1)}, f32[14,384]{1,0:T(8,128)}, u32[]{:S(2)}) copy-start(f32[14,384]{1,0:T(8,128)} %refs_4_.1) | copy-start | bytes 64516
  55.4 13.6 %copy-start.9 = (s32[2,512]{1,0:T(2,128)S(1)}, s32[2,512]{1,0:T(2,128)}, u32[]{:S(2)}) copy-start(s32[2,512]{1,0:T(2,128)} %param.23) | copy-start | bytes 12292
  336.8 10.2 %copy-start.3 = (bf16[192,768]{1,0:T(8,128)(2,1)S(1)}, bf16[192,768]{1,0:T(8,128)(2,1)}, u32[]{:S(2)}) copy-start(bf16[192,768]{1,0:T(8,128)(2,1)} %get-tuple-element.89) | copy-start | bytes 884740
  336.8 10.2 %copy-start.4 = (bf16[192,768]{1,0:T(8,128)(2,1)S(1)}, bf16[192,768]{1,0:T(8,128)(2,1)}, u32[]{:S(2)}) copy-start(bf16[192,768]{1,0:T(8,128)(2,1)} %get-tuple-element.90) | copy-start | bytes 884740
  336.8 10.2 %copy-start.5 = (bf16[192,768]{1,0:T(8,128)(2,1)S(1)}, bf16[192,768]{1,0:T(8,128)(2,1)}, u32[]{:S(2)}) copy-start(bf16[192,768]{1,0:T(8,128)(2,1)} %get-tuple-element.87) | copy-start | bytes 884740
  336.8 10.1 %copy-start.6 = (bf16[192,768]{1,0:T(8,128)(2,1)S(1)}, bf16[192,768]{1,0:T(8,128)(2,1)}, u32[]{:S(2)}) copy-start(bf16[192,768]{1,0:T(8,128)(2,1)} %get-tuple-element.88) | copy-start | bytes 884740
Sparse Core Ops, SparseCore 0:
  10.5 42.1 all-gather.7
  55.1 41.6 all-gather.9
  99.2 39.3 all-gather.5
